TPU v7x, 512 devices: a whole 4x8x8 slice. The times are simulated.
512 devices in a mesh: dp: 32 (over x, y), seq: 16 (over z, core).
Axes of the slice: x: 4, y: 8, z: 8, core: 2. Of those that a mesh axis runs over, the one named last changes fastest.
Arguments:
- tri_query: bfloat16 [65536, 2048], P(('dp', 'seq')), parts along dimension 0, may hold values from -52 to 52
- tri_keys: bfloat16 [65536, 512], P(('dp', 'seq')), parts along dimension 0, may hold values from -4 to 4
- att_query: bfloat16 [65536, 2048], P(('dp', 'seq')), parts along dimension 0, may hold values from -52 to 52
- norm_gain: float32 [2048], replicated, may hold values from 0.1 to 1.9
- kv_weight: bfloat16 [2048, 256], replicated, may hold values from -0.125 to 0.125
Outputs:
- tri_out: bfloat16 [65536, 2048], P(('dp', 'seq')), parts along dimension 0
- attended: bfloat16 [65536, 2048], P(('dp', 'seq')), parts along dimension 0
There are 32 independent parts, one for each index of `dp`. A program takes and returns all parts, laid end to end along the dimension named above; an argument that names none is the same for every part. Nothing has to cross between parts.
All inputs are finite; a program needn't handle non-finite values.
Results may differ from a plain program's by a relative error of at most 0.019.
The roundings to bfloat16 on the way count: a program that leaves them out, or rounds other values in their place, can miss the bound.
Values may be sent and summed in bfloat16 or wider, within the bound.
No kernel may reach another device: no remote copies, remote signals or barrier semaphores. Data moves between devices by JAX's collectives and lax.ppermute only.
A program may use at most 64 MiB of HBM per device.

v0:
```python
import jax
import jax.numpy as jnp
from jax import lax
from jax.sharding import PartitionSpec as P

HEAD_DIM = 128
W1 = 128
W2 = 16


NEG = -1e30


def passed_along(block, axis, distance):
    devices = range(lax.axis_size(axis))
    route = [(i - distance, i) for i in devices if i - distance in devices]
    return lax.ppermute(block, axis, route)


def tri_block(query_rows, window, first_pos):
    head_width = window.shape[1] // 4
    row_count = query_rows.shape[0]
    head_count = query_rows.shape[1] // head_width
    scale = head_width ** (-0.5)
    key_one = window[:, :head_width]
    val_one = window[:, head_width : 2 * head_width]
    key_two = jnp.stack(
        [
            window[row_count - delay : 2 * row_count - delay, 2 * head_width : 3 * head_width]
            for delay in range(W2)
        ]
    ).astype(jnp.float32)
    val_two = jnp.stack(
        [window[row_count - delay : 2 * row_count - delay, 3 * head_width :] for delay in range(W2)]
    ).astype(jnp.float32)
    query_pos = first_pos + jnp.arange(row_count, dtype=jnp.int32)
    key_pos = first_pos - row_count + jnp.arange(2 * row_count, dtype=jnp.int32)
    distance = (
        jnp.arange(2 * row_count, dtype=jnp.int32)[None, :]
        - jnp.arange(row_count, dtype=jnp.int32)[:, None]
    )
    inside = (distance >= 1) & (distance <= row_count) & (key_pos[None, :] >= 0)
    lagged = query_pos[None, :] - jnp.arange(W2, dtype=jnp.int32)[:, None]
    allowed = inside[None, :, :] & (lagged >= 0)[:, :, None]
    per_head = query_rows.reshape(row_count, head_count, head_width).transpose(1, 0, 2)

    def one_head(query):
        mixed_q = (query.astype(jnp.float32)[None] * key_two).astype(jnp.bfloat16)
        score = (
            jnp.einsum("oad,rd->oar", mixed_q, key_one, preferred_element_type=jnp.float32) * scale
        )
        row_top = jnp.max(jnp.where(allowed, score, NEG), axis=(0, 2))
        weight = jnp.where(allowed, jnp.exp(score - row_top[None, :, None]), 0.0)
        row_total = jnp.sum(weight, axis=(0, 2))
        paired = jnp.einsum(
            "oar,rd->oad", weight.astype(jnp.bfloat16), val_one, preferred_element_type=jnp.float32
        )
        return jnp.sum(val_two * paired, axis=0) / row_total[:, None]

    result = lax.map(one_head, per_head)
    return (
        result.transpose(1, 0, 2).reshape(row_count, head_count * head_width).astype(jnp.bfloat16)
    )


def make_fold(queries, first_pos, q_block):
    row_count = queries.shape[0]
    head_count = queries.shape[1] // HEAD_DIM
    shaped = queries.reshape(row_count, head_count, HEAD_DIM)
    scale = HEAD_DIM ** (-0.5)

    def fold_step(carried, kv_piece, begin_at):
        key_rows = kv_piece[:, :HEAD_DIM]
        val_rows = kv_piece[:, HEAD_DIM:]
        key_pos = jnp.arange(kv_piece.shape[0], dtype=jnp.int32)

        def one_block(number, current):
            offset = number * q_block

            def attend(inner):
                row_top, row_total, accum = inner
                query = lax.dynamic_slice_in_dim(shaped, offset, q_block, 0)
                query_pos = first_pos + offset + jnp.arange(q_block, dtype=jnp.int32)
                score = (
                    jnp.einsum("qhe,pe->qhp", query, key_rows, preferred_element_type=jnp.float32)
                    * scale
                )
                allowed = key_pos[None, None, :] <= query_pos[:, None, None]
                old_top = lax.dynamic_slice_in_dim(row_top, offset, q_block, 0)
                old_total = lax.dynamic_slice_in_dim(row_total, offset, q_block, 0)
                old_accum = lax.dynamic_slice_in_dim(accum, offset, q_block, 0)
                new_top = jnp.maximum(old_top, jnp.max(jnp.where(allowed, score, NEG), -1))
                weight = jnp.where(allowed, jnp.exp(score - new_top[..., None]), 0.0)
                rescale = jnp.exp(old_top - new_top)
                new_total = old_total * rescale + jnp.sum(weight, -1)
                new_accum = old_accum * rescale[..., None] + jnp.einsum(
                    "qhp,pe->qhe",
                    weight.astype(jnp.bfloat16),
                    val_rows,
                    preferred_element_type=jnp.float32,
                )
                return (
                    lax.dynamic_update_slice_in_dim(row_top, new_top, offset, 0),
                    lax.dynamic_update_slice_in_dim(row_total, new_total, offset, 0),
                    lax.dynamic_update_slice_in_dim(accum, new_accum, offset, 0),
                )

            return lax.cond(
                first_pos + offset + q_block - 1 >= begin_at, attend, lambda inner: inner, current
            )

        return lax.fori_loop(0, row_count // q_block, one_block, carried)

    initial = (
        jnp.full((row_count, head_count), NEG, jnp.float32),
        jnp.zeros((row_count, head_count), jnp.float32),
        jnp.zeros((row_count, head_count, HEAD_DIM), jnp.float32),
    )
    return (fold_step, initial)


def finish(carried):
    row_top, row_total, accum = carried
    result = accum / row_total[..., None]
    return result.reshape(result.shape[0], result.shape[1] * HEAD_DIM).astype(jnp.bfloat16)


def per_device(tri_query, tri_keys, att_query, norm_gain, kv_weight):
    tok_rows = tri_query.shape[0]
    anchor = lax.axis_index("seq") * tok_rows
    behind = passed_along(tri_keys, "seq", 1)
    whole = jnp.concatenate([behind, tri_keys], 0)

    def do_block(number):
        begin_at = number * W1
        return tri_block(tri_query, whole, anchor + begin_at)

    tri_out = lax.map(do_block, jnp.arange(tok_rows // W1, dtype=jnp.int32)).reshape(
        tok_rows, tri_query.shape[1]
    )
    widened = tri_out.astype(jnp.float32)
    normed = (
        widened * lax.rsqrt(jnp.mean(widened * widened, -1, keepdims=True) + 1e-06) * norm_gain
    ).astype(jnp.bfloat16)
    key_vals = jnp.dot(normed, kv_weight, preferred_element_type=jnp.float32).astype(jnp.bfloat16)
    head_queries = lax.all_to_all(att_query, "seq", split_axis=1, concat_axis=0, tiled=True)
    fold_step, initial = make_fold(head_queries, 0, min(512, head_queries.shape[0]))
    carried = fold_step(initial, lax.all_gather(key_vals, "seq", axis=0, tiled=True), jnp.int32(0))
    attended = lax.all_to_all(finish(carried), "seq", split_axis=0, concat_axis=1, tiled=True)
    return (tri_out, attended)


def solution(mesh):
    in_specs = (P(("dp", "seq"), None), P(("dp", "seq"), None), P(("dp", "seq"), None), P(), P())
    out_specs = (P(("dp", "seq"), None), P(("dp", "seq"), None))
    return jax.shard_map(
        per_device, mesh=mesh, in_specs=in_specs, out_specs=out_specs, check_vma=False
    )
```

profile of v0, /device:TPU:1, one launch (start us, length us, event | category | flops | bytes accessed | tf_op | source)
XLA Modules:
  0.0 166.1 jit_solution(13219836533437436460)
XLA Ops:
  7.2 5.5 %collective-permute-start = (bf16[128,512]{1,0:T(8,128)(2,1)}, bf16[128,512]{1,0:T(8,128)(2,1)S(1)}, u32[]{:S(2)}, u32[]{:S(2)}) collective-permute-start(bf16[128,512]{1,0:T(8,128)(2,1)} %param.12), channel_id=1, source_target_pairs={{0,1},{1,2},{2,3},{3,4},{4,5},{5,6},{6,7},{7,8},{8,9},{9,10},{10,1... | collective-permute-start | bytes 393224 | tf_op jit(solution)/shard_map/ppermute | solution.py:17
  13.6 1.3 copy.25
  15.0 1.6 collective-permute-done
  16.6 0.9 constant_dynamic-update-slice_fusion.1
  18.0 1.1 convert_element_type.66
  19.2 1.1 convert_element_type.65
  20.3 46.6 %while.40 = (s32[]{:T(128)}, bf16[16,128,128]{2,1,0:T(8,128)(2,1)S(1)}, bf16[16,128,128]{1,2,0:T(8,128)(2,1)S(1)}, f32[16,128,128]{2,1,0:T(8,128)S(1)}, bf16[256...) while((s32[]{:T(128)}, ...), condition=%wide.region_4.5_spmd.clone, body=%wide.region_0.4_spmd.clone.sunk | while | flops 276840192 | bytes 13312657 | solution.py:60
  21.3 0.9 fusion.65
  24.2 0.9 fusion.65
  27.1 0.9 fusion.65
  30.0 0.9 fusion.65
  32.9 0.9 fusion.65
  35.8 0.9 fusion.65
  38.7 0.9 fusion.65
  41.7 0.9 fusion.65
  44.6 0.9 fusion.65
  47.5 0.9 fusion.65
  50.4 0.9 fusion.65
  53.3 0.9 fusion.65
  56.2 0.9 fusion.65
  59.1 0.9 fusion.65
  62.0 0.9 fusion.65
  65.0 0.9 fusion.65
  67.2 1.0 convolution_convert_fusion
  68.3 2.0 %copy.28 = bf16[128,2048]{0,1:T(8,128)(2,1)} copy(bf16[128,2048]{1,0:T(8,128)(2,1)} %param.13) | data formatting | bytes 1048576 | tf_op args[2]
  70.3 10.3 %all-to-all-start = ((bf16[128,16,128]{0,2,1:T(8,128)(2,1)}), bf16[128,16,128]{0,2,1:T(8,128)(2,1)S(1)}, u32[]{:S(2)}, u32[]{:S(2)}) async-start(bf16[128,16,128]{0,2,1:T(8,128)(2,1)} %bitcast.41), calls=%async_computation | async-start | bytes 1048576 | tf_op jit(solution)/shard_map/all_to_all | solution.py:146
  80.6 18.8 %all-to-all-done = bf16[128,16,128]{0,2,1:T(8,128)(2,1)S(1)} async-done(((bf16[128,16,128]{0,2,1:T(8,128)(2,1)}), bf16[128,16,128]{0,2,1:T(8,128)(2,1)S(1)}, u32[]{:S(2)}, u32[]{:S(2)}) %all-to-all-start) | async-done | bytes 524320 | tf_op jit(solution)/shard_map/all_to_all | solution.py:146
  99.7 15.9 %all-gather.2.cloned.1.call-done = bf16[2048,256]{1,0:T(8,128)(2,1)} async-done(((bf16[128,256]{1,0:T(8,128)(2,1)}), bf16[2048,256]{1,0:T(8,128)(2,1)}) %all-gather.2.cloned.1.call-update) | async-done | bytes 1048592 | tf_op jit(solution)/shard_map/all_gather | solution.py:148
  115.6 2.2 %fusion.49 = (bf16[2048,128]{1,0:T(8,128)(2,1)}, bf16[2048,128]{1,0:T(8,128)(2,1)}) fusion(bf16[2048,256]{1,0:T(8,128)(2,1)} %all-gather.2.cloned.1.call-done), kind=kLoop, calls=%fused_computation.127 | loop fusion | bytes 2097152 | tf_op jit(solution)/shard_map/slice | solution.py:74
  118.0 17.6 %while.41 = (s32[]{:T(128)}, f32[2048,1]{0,1:T(1,128)S(1)}, f32[2048,1]{0,1:T(1,128)S(1)}, f32[2048,1,128]{2,0,1:T(8,128)S(1)}, bf16[2048,1,128]{2,0,1:T(8,128)(...) while((s32[]{:T(128)}, f32[2048,1]{0,1:T(1,128)S(1)}, ...), condition=%wide.region_11.12_spmd.clone, body=%wide.region_6.11_spmd.clone.sunk | while | flops 551683584 | bytes 16488797 | solution.py:112
  118.0 4.4 %conditional.3 = ((f32[2048,1]{0,1:T(1,128)S(1)}, f32[2048,1]{0,1:T(1,128)S(1)}, f32[2048,1,128]{2,0,1:T(8,128)S(1)})) conditional(s32[]{:T(128)} %convert_element_type.107, (f32[2048,1]{0,1:T(1,128)S(1)}, f32[2048,1]{0,1:T(1,128)S(1)}, f32[2048,1,128]{2,0,1:T(8,128)S(1)}) %tuple.109, (s32[]{:T(128)}, f32[2048,1]{0,1:T(1,128)S(1)}, ...), branch_computations={%region_7.7_spmd, %region_8.10_spmd} | conditional | flops 551683584 | bytes 16480370 | solution.py:108
  118.1 2.1 %fusion.4 = (f32[512]{0:T(512)S(1)}, f32[512,2048]{1,0:T(8,128)S(1)}) fusion(s32[2048]{0:T(1024)S(1)} %get-tuple-element.354, s32[512]{0:T(512)S(1)} %iota_add_fusion, bf16[2048,128]{1,0:T(8,128)(2,1)} %get-tuple-element.356, bf16[2048,1,128]{2,0,1:T(8,128)(2,1)S(1)} %get-tuple-element.355, s32[]{:T(128)S(6)} %select_n.22), kind=kOutput, calls=%fused_computation.4 | convolution fusion | flops 272629248 | bytes 4861956 | tf_op jit(solution)/shard_map/while/body/eval_jaxpr/cond/branch_1_fun/qhe,pe->qhp/dot_general | solution.py:85
  120.1 1.1 fusion.6
  121.3 1.1 fusion.15
  122.4 4.4 %conditional.3 = ((f32[2048,1]{0,1:T(1,128)S(1)}, f32[2048,1]{0,1:T(1,128)S(1)}, f32[2048,1,128]{2,0,1:T(8,128)S(1)})) conditional(s32[]{:T(128)} %convert_element_type.107, (f32[2048,1]{0,1:T(1,128)S(1)}, f32[2048,1]{0,1:T(1,128)S(1)}, f32[2048,1,128]{2,0,1:T(8,128)S(1)}) %tuple.109, (s32[]{:T(128)}, f32[2048,1]{0,1:T(1,128)S(1)}, ...), branch_computations={%region_7.7_spmd, %region_8.10_spmd} | conditional | flops 551683584 | bytes 16480370 | solution.py:108
  122.5 2.1 %fusion.4 = (f32[512]{0:T(512)S(1)}, f32[512,2048]{1,0:T(8,128)S(1)}) fusion(s32[2048]{0:T(1024)S(1)} %get-tuple-element.354, s32[512]{0:T(512)S(1)} %iota_add_fusion, bf16[2048,128]{1,0:T(8,128)(2,1)} %get-tuple-element.356, bf16[2048,1,128]{2,0,1:T(8,128)(2,1)S(1)} %get-tuple-element.355, s32[]{:T(128)S(6)} %select_n.22), kind=kOutput, calls=%fused_computation.4 | convolution fusion | flops 272629248 | bytes 4861956 | tf_op jit(solution)/shard_map/while/body/eval_jaxpr/cond/branch_1_fun/qhe,pe->qhp/dot_general | solution.py:85
  124.5 1.1 fusion.6
  125.7 1.1 fusion.15
  126.8 4.4 %conditional.3 = ((f32[2048,1]{0,1:T(1,128)S(1)}, f32[2048,1]{0,1:T(1,128)S(1)}, f32[2048,1,128]{2,0,1:T(8,128)S(1)})) conditional(s32[]{:T(128)} %convert_element_type.107, (f32[2048,1]{0,1:T(1,128)S(1)}, f32[2048,1]{0,1:T(1,128)S(1)}, f32[2048,1,128]{2,0,1:T(8,128)S(1)}) %tuple.109, (s32[]{:T(128)}, f32[2048,1]{0,1:T(1,128)S(1)}, ...), branch_computations={%region_7.7_spmd, %region_8.10_spmd} | conditional | flops 551683584 | bytes 16480370 | solution.py:108
  126.8 2.1 %fusion.4 = (f32[512]{0:T(512)S(1)}, f32[512,2048]{1,0:T(8,128)S(1)}) fusion(s32[2048]{0:T(1024)S(1)} %get-tuple-element.354, s32[512]{0:T(512)S(1)} %iota_add_fusion, bf16[2048,128]{1,0:T(8,128)(2,1)} %get-tuple-element.356, bf16[2048,1,128]{2,0,1:T(8,128)(2,1)S(1)} %get-tuple-element.355, s32[]{:T(128)S(6)} %select_n.22), kind=kOutput, calls=%fused_computation.4 | convolution fusion | flops 272629248 | bytes 4861956 | tf_op jit(solution)/shard_map/while/body/eval_jaxpr/cond/branch_1_fun/qhe,pe->qhp/dot_general | solution.py:85
  128.9 1.1 fusion.6
  130.1 1.1 fusion.15
  131.2 4.4 %conditional.3 = ((f32[2048,1]{0,1:T(1,128)S(1)}, f32[2048,1]{0,1:T(1,128)S(1)}, f32[2048,1,128]{2,0,1:T(8,128)S(1)})) conditional(s32[]{:T(128)} %convert_element_type.107, (f32[2048,1]{0,1:T(1,128)S(1)}, f32[2048,1]{0,1:T(1,128)S(1)}, f32[2048,1,128]{2,0,1:T(8,128)S(1)}) %tuple.109, (s32[]{:T(128)}, f32[2048,1]{0,1:T(1,128)S(1)}, ...), branch_computations={%region_7.7_spmd, %region_8.10_spmd} | conditional | flops 551683584 | bytes 16480370 | solution.py:108
  131.2 2.1 %fusion.4 = (f32[512]{0:T(512)S(1)}, f32[512,2048]{1,0:T(8,128)S(1)}) fusion(s32[2048]{0:T(1024)S(1)} %get-tuple-element.354, s32[512]{0:T(512)S(1)} %iota_add_fusion, bf16[2048,128]{1,0:T(8,128)(2,1)} %get-tuple-element.356, bf16[2048,1,128]{2,0,1:T(8,128)(2,1)S(1)} %get-tuple-element.355, s32[]{:T(128)S(6)} %select_n.22), kind=kOutput, calls=%fused_computation.4 | convolution fusion | flops 272629248 | bytes 4861956 | tf_op jit(solution)/shard_map/while/body/eval_jaxpr/cond/branch_1_fun/qhe,pe->qhp/dot_general | solution.py:85
  133.3 1.1 fusion.6
  134.5 1.1 fusion.15
  135.9 22.0 %all_to_all.32 = bf16[16,128,128]{2,1,0:T(8,128)(2,1)S(1)} all-to-all(bf16[16,128,128]{2,1,0:T(8,128)(2,1)S(1)} %bitcast.184), channel_id=1, replica_groups=mesh['dp'=32,'seq'=16] {'seq'}, dimensions={0} | all-to-all | bytes 1048576 | tf_op jit(solution)/shard_map/all_to_all | solution.py:149
  158.2 1.0 copy.31
  (202 shorter events, 33.6 us)
Async XLA Ops:
  7.2 60.1 %copy-start = (bf16[2048,256]{1,0:T(8,128)(2,1)S(1)}, bf16[2048,256]{1,0:T(8,128)(2,1)}, u32[]{:S(2)}) copy-start(bf16[2048,256]{1,0:T(8,128)(2,1)} %param.15) | copy-start | bytes 3145732
  7.2 108.4 %all-gather.2.cloned.1.call-start = ((), (), s32[]{:S(2)}) async-start(), calls=%async_computation.2 | async-start | bytes 1114112 | tf_op jit(solution)/shard_map/all_gather | solution.py:148
  7.2 9.3 %collective-permute-start = (bf16[128,512]{1,0:T(8,128)(2,1)}, bf16[128,512]{1,0:T(8,128)(2,1)S(1)}, u32[]{:S(2)}, u32[]{:S(2)}) collective-permute-start(bf16[128,512]{1,0:T(8,128)(2,1)} %param.12), channel_id=1, source_target_pairs={{0,1},{1,2},{2,3},{3,4},{4,5},{5,6},{6,7},{7,8},{8,9},{9,10},{10,1... | collective-permute-start | bytes 393224 | tf_op jit(solution)/shard_map/ppermute | solution.py:17
  18.0 1.2 copy-start.2
  20.3 46.9 %copy-start.5 = (f32[2048]{0:T(1024)S(1)}, f32[2048]{0:T(1024)}, u32[]{:S(2)}) copy-start(f32[2048]{0:T(1024)} %param.14) | copy-start | bytes 24580
  20.5 1.7 %copy-start.1 = (f32[16,128,128]{2,1,0:T(8,128)S(1)}, f32[16,128,128]{2,1,0:T(8,128)}, u32[]{:S(2)}) copy-start(f32[16,128,128]{2,1,0:T(8,128)} %get-tuple-element.675) | copy-start | bytes 3145732 | tf_op jit(solution)/shard_map/while/body/eval_jaxpr/while
  23.4 1.7 %copy-start.1 = (f32[16,128,128]{2,1,0:T(8,128)S(1)}, f32[16,128,128]{2,1,0:T(8,128)}, u32[]{:S(2)}) copy-start(f32[16,128,128]{2,1,0:T(8,128)} %get-tuple-element.675) | copy-start | bytes 3145732 | tf_op jit(solution)/shard_map/while/body/eval_jaxpr/while
  26.3 1.7 %copy-start.1 = (f32[16,128,128]{2,1,0:T(8,128)S(1)}, f32[16,128,128]{2,1,0:T(8,128)}, u32[]{:S(2)}) copy-start(f32[16,128,128]{2,1,0:T(8,128)} %get-tuple-element.675) | copy-start | bytes 3145732 | tf_op jit(solution)/shard_map/while/body/eval_jaxpr/while
  29.2 1.7 %copy-start.1 = (f32[16,128,128]{2,1,0:T(8,128)S(1)}, f32[16,128,128]{2,1,0:T(8,128)}, u32[]{:S(2)}) copy-start(f32[16,128,128]{2,1,0:T(8,128)} %get-tuple-element.675) | copy-start | bytes 3145732 | tf_op jit(solution)/shard_map/while/body/eval_jaxpr/while
  32.1 1.7 %copy-start.1 = (f32[16,128,128]{2,1,0:T(8,128)S(1)}, f32[16,128,128]{2,1,0:T(8,128)}, u32[]{:S(2)}) copy-start(f32[16,128,128]{2,1,0:T(8,128)} %get-tuple-element.675) | copy-start | bytes 3145732 | tf_op jit(solution)/shard_map/while/body/eval_jaxpr/while
  35.0 1.7 %copy-start.1 = (f32[16,128,128]{2,1,0:T(8,128)S(1)}, f32[16,128,128]{2,1,0:T(8,128)}, u32[]{:S(2)}) copy-start(f32[16,128,128]{2,1,0:T(8,128)} %get-tuple-element.675) | copy-start | bytes 3145732 | tf_op jit(solution)/shard_map/while/body/eval_jaxpr/while
  37.9 1.7 %copy-start.1 = (f32[16,128,128]{2,1,0:T(8,128)S(1)}, f32[16,128,128]{2,1,0:T(8,128)}, u32[]{:S(2)}) copy-start(f32[16,128,128]{2,1,0:T(8,128)} %get-tuple-element.675) | copy-start | bytes 3145732 | tf_op jit(solution)/shard_map/while/body/eval_jaxpr/while
  40.9 1.7 %copy-start.1 = (f32[16,128,128]{2,1,0:T(8,128)S(1)}, f32[16,128,128]{2,1,0:T(8,128)}, u32[]{:S(2)}) copy-start(f32[16,128,128]{2,1,0:T(8,128)} %get-tuple-element.675) | copy-start | bytes 3145732 | tf_op jit(solution)/shard_map/while/body/eval_jaxpr/while
  43.8 1.7 %copy-start.1 = (f32[16,128,128]{2,1,0:T(8,128)S(1)}, f32[16,128,128]{2,1,0:T(8,128)}, u32[]{:S(2)}) copy-start(f32[16,128,128]{2,1,0:T(8,128)} %get-tuple-element.675) | copy-start | bytes 3145732 | tf_op jit(solution)/shard_map/while/body/eval_jaxpr/while
  46.7 1.7 %copy-start.1 = (f32[16,128,128]{2,1,0:T(8,128)S(1)}, f32[16,128,128]{2,1,0:T(8,128)}, u32[]{:S(2)}) copy-start(f32[16,128,128]{2,1,0:T(8,128)} %get-tuple-element.675) | copy-start | bytes 3145732 | tf_op jit(solution)/shard_map/while/body/eval_jaxpr/while
  49.6 1.7 %copy-start.1 = (f32[16,128,128]{2,1,0:T(8,128)S(1)}, f32[16,128,128]{2,1,0:T(8,128)}, u32[]{:S(2)}) copy-start(f32[16,128,128]{2,1,0:T(8,128)} %get-tuple-element.675) | copy-start | bytes 3145732 | tf_op jit(solution)/shard_map/while/body/eval_jaxpr/while
  52.5 1.7 %copy-start.1 = (f32[16,128,128]{2,1,0:T(8,128)S(1)}, f32[16,128,128]{2,1,0:T(8,128)}, u32[]{:S(2)}) copy-start(f32[16,128,128]{2,1,0:T(8,128)} %get-tuple-element.675) | copy-start | bytes 3145732 | tf_op jit(solution)/shard_map/while/body/eval_jaxpr/while
  55.4 1.7 %copy-start.1 = (f32[16,128,128]{2,1,0:T(8,128)S(1)}, f32[16,128,128]{2,1,0:T(8,128)}, u32[]{:S(2)}) copy-start(f32[16,128,128]{2,1,0:T(8,128)} %get-tuple-element.675) | copy-start | bytes 3145732 | tf_op jit(solution)/shard_map/while/body/eval_jaxpr/while
  58.3 1.7 %copy-start.1 = (f32[16,128,128]{2,1,0:T(8,128)S(1)}, f32[16,128,128]{2,1,0:T(8,128)}, u32[]{:S(2)}) copy-start(f32[16,128,128]{2,1,0:T(8,128)} %get-tuple-element.675) | copy-start | bytes 3145732 | tf_op jit(solution)/shard_map/while/body/eval_jaxpr/while
  61.2 1.7 %copy-start.1 = (f32[16,128,128]{2,1,0:T(8,128)S(1)}, f32[16,128,128]{2,1,0:T(8,128)}, u32[]{:S(2)}) copy-start(f32[16,128,128]{2,1,0:T(8,128)} %get-tuple-element.675) | copy-start | bytes 3145732 | tf_op jit(solution)/shard_map/while/body/eval_jaxpr/while
  64.2 1.7 %copy-start.1 = (f32[16,128,128]{2,1,0:T(8,128)S(1)}, f32[16,128,128]{2,1,0:T(8,128)}, u32[]{:S(2)}) copy-start(f32[16,128,128]{2,1,0:T(8,128)} %get-tuple-element.675) | copy-start | bytes 3145732 | tf_op jit(solution)/shard_map/while/body/eval_jaxpr/while
  67.2 50.8 %copy-start.3 = (bf16[128,2048]{1,0:T(8,128)(2,1)}, bf16[128,2048]{1,0:T(8,128)(2,1)S(1)}, u32[]{:S(2)}) copy-start(bf16[128,2048]{1,0:T(8,128)(2,1)S(1)} %copy_bitcast_fusion) | copy-start | bytes 1572868
  70.3 29.1 %all-to-all-start = ((bf16[128,16,128]{0,2,1:T(8,128)(2,1)}), bf16[128,16,128]{0,2,1:T(8,128)(2,1)S(1)}, u32[]{:S(2)}, u32[]{:S(2)}) async-start(bf16[128,16,128]{0,2,1:T(8,128)(2,1)} %bitcast.41), calls=%async_computation | async-start | bytes 1048576 | tf_op jit(solution)/shard_map/all_to_all | solution.py:146
  118.0 3.2 %copy-start.4 = (bf16[2048,128]{1,0:T(8,128)(2,1)S(1)}, bf16[2048,128]{1,0:T(8,128)(2,1)}, u32[]{:S(2)}) copy-start(bf16[2048,128]{1,0:T(8,128)(2,1)} %get-tuple-element.359) | copy-start | bytes 1572868 | tf_op jit(solution)/shard_map/while/body/eval_jaxpr/cond
  122.4 3.2 %copy-start.4 = (bf16[2048,128]{1,0:T(8,128)(2,1)S(1)}, bf16[2048,128]{1,0:T(8,128)(2,1)}, u32[]{:S(2)}) copy-start(bf16[2048,128]{1,0:T(8,128)(2,1)} %get-tuple-element.359) | copy-start | bytes 1572868 | tf_op jit(solution)/shard_map/while/body/eval_jaxpr/cond
  126.8 3.2 %copy-start.4 = (bf16[2048,128]{1,0:T(8,128)(2,1)S(1)}, bf16[2048,128]{1,0:T(8,128)(2,1)}, u32[]{:S(2)}) copy-start(bf16[2048,128]{1,0:T(8,128)(2,1)} %get-tuple-element.359) | copy-start | bytes 1572868 | tf_op jit(solution)/shard_map/while/body/eval_jaxpr/cond
  131.2 3.2 %copy-start.4 = (bf16[2048,128]{1,0:T(8,128)(2,1)S(1)}, bf16[2048,128]{1,0:T(8,128)(2,1)}, u32[]{:S(2)}) copy-start(bf16[2048,128]{1,0:T(8,128)(2,1)} %get-tuple-element.359) | copy-start | bytes 1572868 | tf_op jit(solution)/shard_map/while/body/eval_jaxpr/cond
Sparse Core Ops, SparseCore 0:
  68.4 47.1 all-gather.1
where the time goes:
time: 167 us; the launch traced here: 166 us
  matrix products  40.5 us (24%)
  waiting for transfers between devices  36.3 us (22%)
  other arithmetic  24 us (14%)
  blocking collectives  22 us (13%)
  starting transfers between devices  15.9 us (10%)
  between operations  14.2 us (9%)
  local copies, waits for them, and re-layouts  11.6 us (7%)
    all_to_all x1, blocking collectives, per_device(): lax.all_to_all(finish(carried), 'seq', split_axis=0, concat_axis=1, tiled...  22 us
    all_to_all x1, waiting for transfers between devices, per_device(): lax.all_to_all(att_query, 'seq', split_axis=1, concat_axis=0, tiled=True)  18.8 us
    all_gather x1, waiting for transfers between devices, per_device(): lax.all_gather(key_vals, 'seq', axis=0, tiled=True)  15.9 us
    reduce_sum x16, other arithmetic, one_head(): row_total = jnp.sum(weight, axis=(0, 2))  14.8 us
    dot_general x16, matrix products, one_head(): jnp.einsum('oar,rd->oad', weight.astype(jnp.bfloat16), val_one, preferred...  14.7 us
    dot_general x16, matrix products, one_head(): jnp.einsum('oad,rd->oar', mixed_q, key_one, preferred_element_type=jnp.fl...  12.3 us
    all_to_all x1, starting transfers between devices, per_device(): lax.all_to_all(att_query, 'seq', split_axis=1, concat_axis=0, tiled=True)  10.3 us
    dot_general x4, matrix products, attend(): jnp.einsum('qhe,pe->qhp', query, key_rows, preferred_element_type=jnp.flo...  8.22 us
  transfers between devices with their start and end apart: 3, of which 3 were waited for; matrix products, arithmetic and copies ran while one was open for 3% of the time, Pallas kernels for 0%

commit v1 on v0

v1 whole, which is shorter than its diff:
```python
import functools

import jax
import jax.numpy as jnp
from jax import lax
from jax.experimental import pallas as pl
from jax.experimental.pallas import tpu as pltpu
from jax.sharding import PartitionSpec as P

HEADS = 16
DIM = 128
W1 = 128
W2 = 16
NEG = -1e30
SCALE = DIM**-0.5
EXP2_SCALE = SCALE * 1.4426950408889634
NT = (((1,), (1,)), ((), ()))


def tri_kernel(
    me_ref, q_ref, prev_ref, cur_ref, gain_ref, weight_ref, held_ref, out_ref, kv_ref,
    k2_scr, v2_scr, mask_scr, mq_scr, s_scr, normed_scr, shift_scr, *, first_row, rows,
):
    first_shard = me_ref[0] == 0

    shift_scr[0:16, :] = prev_ref[W1 - 16 : W1, 2 * DIM :].astype(jnp.float32)
    shift_scr[16:, :] = cur_ref[:, 2 * DIM :].astype(jnp.float32)
    for lag in range(W2):
        at = 16 + first_row - lag
        k2_scr[lag] = shift_scr[at : at + rows, :DIM].astype(jnp.bfloat16)
        v2_scr[lag] = shift_scr[at : at + rows, DIM:]
    row = first_row + lax.broadcasted_iota(jnp.int32, (rows, DIM), 0)
    col = lax.broadcasted_iota(jnp.int32, (rows, DIM), 1)
    own = col <= row
    mask_scr[0] = jnp.where(own, 1.0, 0.0).astype(jnp.bfloat16)
    k1 = jnp.concatenate([cur_ref[:, :DIM], prev_ref[:, :DIM]], 0)
    v1 = jnp.concatenate([cur_ref[:, DIM : 2 * DIM], prev_ref[:, DIM : 2 * DIM]], 0)

    def one_head(head, square, first):
        lanes = pl.ds(pl.multiple_of(head * DIM, DIM), DIM)
        query = q_ref[:, lanes]
        mq = (query[None] * k2_scr[...]).reshape(W2 * rows, DIM)
        both = lax.dot_general(mq, k1, NT, preferred_element_type=jnp.float32)
        both = both.reshape(W2, rows, 2 * DIM)
        if first:
            score = jnp.where(own[None], both[:, :, :DIM], NEG)
            if first_row < W2:
                lag = lax.broadcasted_iota(jnp.int32, (W2, rows, DIM), 0)
                score = jnp.where(lag <= row[None], score, NEG)
        else:
            score = jnp.where(own[None], both[:, :, :DIM], both[:, :, DIM:])
        s_scr[...] = score
        top = jnp.max(jnp.max(score, axis=0), axis=-1, keepdims=True)
        weight = jnp.exp2((s_scr[...] - top[None]) * EXP2_SCALE)
        total = jnp.sum(jnp.sum(weight, axis=0), axis=-1, keepdims=True)
        rounded = weight.astype(jnp.bfloat16)
        w_own = rounded * mask_scr[...]
        w_prev = rounded - w_own
        halves = jnp.concatenate([w_own, w_prev], -1).reshape(W2 * rows, 2 * DIM)
        paired = jnp.dot(halves, v1, preferred_element_type=jnp.float32)
        result = jnp.sum(paired.reshape(W2, rows, DIM) * v2_scr[...], axis=0) / total
        result = result.astype(jnp.bfloat16)
        out_ref[:, lanes] = result
        wide = result.astype(jnp.float32)
        return square + wide * wide

    def finish(square):
        mean = jnp.sum(square, axis=-1, keepdims=True) * (1.0 / (HEADS * DIM))
        inverse = lax.rsqrt(mean + 1e-6)
        normed = (out_ref[...].astype(jnp.float32) * inverse * gain_ref[...]).astype(jnp.bfloat16)
        kv_ref[...] = jnp.dot(
            normed, weight_ref[...], preferred_element_type=jnp.float32
        ).astype(jnp.bfloat16)

    zero = jnp.zeros((rows, DIM), jnp.float32)

    @pl.when(first_shard)
    def _():
        finish(lax.fori_loop(0, HEADS, lambda h, sq: one_head(h, sq, True), zero))

    @pl.when(jnp.logical_not(first_shard))
    def _():
        finish(lax.fori_loop(0, HEADS, lambda h, sq: one_head(h, sq, False), zero))


def tri_call(me, tri_query, behind, tri_keys, gain, kv_weight, held, number, rows):
    token_rows, width = tri_query.shape
    whole = lambda shape: pl.BlockSpec(shape, lambda i: (0,) * len(shape))
    in_specs = [
        pl.BlockSpec(memory_space=pltpu.SMEM),
        pl.BlockSpec((rows, width), lambda i: (number, 0)),
        whole(behind.shape),
        whole(tri_keys.shape),
        whole(gain.shape),
        whole(kv_weight.shape),
    ]
    args = [me, tri_query, behind, tri_keys, gain, kv_weight]
    body = functools.partial(tri_kernel, first_row=number * rows, rows=rows)
    aliases = {}
    if held is None:
        kernel = lambda *refs: body(*refs[:6], None, *refs[6:])
    else:
        kernel = body
        in_specs.append(pl.BlockSpec(memory_space=pl.ANY))
        args.append(held)
        aliases = {6: 0}
    return pl.pallas_call(
        kernel,
        grid=(1,),
        in_specs=in_specs,
        out_specs=[
            pl.BlockSpec((rows, width), lambda i: (number, 0)),
            whole((rows, 2 * DIM)),
        ],
        out_shape=[
            jax.ShapeDtypeStruct((token_rows, width), jnp.bfloat16),
            jax.ShapeDtypeStruct((rows, 2 * DIM), jnp.bfloat16),
        ],
        scratch_shapes=[
            pltpu.VMEM((W2, rows, DIM), jnp.bfloat16),
            pltpu.VMEM((W2, rows, DIM), jnp.float32),
            pltpu.VMEM((1, rows, DIM), jnp.bfloat16),
            pltpu.VMEM((W2, rows, DIM), jnp.bfloat16),
            pltpu.VMEM((W2, rows, DIM), jnp.float32),
            pltpu.VMEM((rows, width), jnp.bfloat16),
            pltpu.VMEM((W1 + 16, 2 * DIM), jnp.float32),
        ],
        input_output_aliases=aliases,
        compiler_params=pltpu.CompilerParams(vmem_limit_bytes=40 * 1024 * 1024),
        cost_estimate=pl.CostEstimate(
            flops=4 * rows * HEADS * W2 * 256 * DIM, bytes_accessed=2 << 20, transcendentals=0
        ),
        name="tri_part",
    )(*args)


def att_kernel(me_ref, q_ref, far_ref, own_ref, out_ref, q_scr, k_scr, v_scr, s_scr, top_scr, total_scr, acc_scr, *, rows, step, group):
    me = me_ref[0]
    far = far_ref.shape[0]
    tokens = k_scr.shape[0]
    k_scr[:far, :] = far_ref[:, :DIM]
    v_scr[:far, :] = far_ref[:, DIM:]
    if far < tokens:
        k_scr[far:, :] = jnp.zeros((tokens - far, DIM), jnp.bfloat16)
        v_scr[far:, :] = jnp.zeros((tokens - far, DIM), jnp.bfloat16)
    here = pl.ds(pl.multiple_of(me * rows, rows), rows)
    k_scr[here, :] = own_ref[:, :DIM]
    v_scr[here, :] = own_ref[:, DIM:]
    full = (me * rows) // step
    size = group * rows

    def one_group(g, _):
        for h in range(group):
            lanes = pl.ds(pl.multiple_of((g * group + h) * DIM, DIM), DIM)
            q_scr[h * rows : (h + 1) * rows, :] = q_ref[:, lanes]
        top_scr[...] = jnp.full((size, DIM), NEG, jnp.float32)

        def scores(b):
            keys = k_scr[pl.ds(pl.multiple_of(b * step, step), step), :]
            return lax.dot_general(q_scr[...], keys, NT, preferred_element_type=jnp.float32)

        def keep(b, score):
            s_scr[b] = score
            top = top_scr[...]
            for c in range(step // DIM):
                top = jnp.maximum(top, score[:, c * DIM : (c + 1) * DIM])
            top_scr[...] = top

        def first_pass(b, _):
            keep(b, scores(b))
            return 0

        lax.fori_loop(0, full, first_pass, 0)
        key_pos = full * step + lax.broadcasted_iota(jnp.int32, (rows, step), 1)
        query_pos = me * rows + lax.broadcasted_iota(jnp.int32, (rows, step), 0)
        last = scores(full).reshape(group, rows, step)
        last = jnp.where((key_pos <= query_pos)[None], last, NEG).reshape(size, step)
        keep(full, last)
        top = jnp.max(top_scr[...], axis=-1, keepdims=True)
        top_scr[...] = jnp.broadcast_to(top, (size, DIM))
        total_scr[...] = jnp.zeros((size, DIM), jnp.float32)
        acc_scr[...] = jnp.zeros((size, DIM), jnp.float32)

        def second_pass(b, _):
            values = v_scr[pl.ds(pl.multiple_of(b * step, step), step), :]
            top = top_scr[...]
            weights = []
            total = total_scr[...]
            for c in range(step // DIM):
                weight = jnp.exp2((s_scr[b, :, c * DIM : (c + 1) * DIM] - top) * EXP2_SCALE)
                total = total + weight
                weights.append(weight.astype(jnp.bfloat16))
            total_scr[...] = total
            acc_scr[...] += jnp.dot(
                jnp.concatenate(weights, -1), values, preferred_element_type=jnp.float32
            )
            return 0

        lax.fori_loop(0, full + 1, second_pass, 0)
        result = acc_scr[...] / jnp.sum(total_scr[...], axis=-1, keepdims=True)
        result = result.astype(jnp.bfloat16)
        for h in range(group):
            lanes = pl.ds(pl.multiple_of((g * group + h) * DIM, DIM), DIM)
            out_ref[:, lanes] = result[h * rows : (h + 1) * rows, :]
        return 0

    lax.fori_loop(0, HEADS // group, one_group, 0)


def att_call(me, att_query, far, own, step=256, group=4):
    rows, width = att_query.shape
    tokens = 16 * rows
    size = group * rows
    whole = lambda shape: pl.BlockSpec(shape, lambda i: (0,) * len(shape))
    return pl.pallas_call(
        functools.partial(att_kernel, rows=rows, step=step, group=group),
        grid=(1,),
        in_specs=[
            pl.BlockSpec(memory_space=pltpu.SMEM),
            whole(att_query.shape),
            whole(far.shape),
            whole(own.shape),
        ],
        out_specs=whole(att_query.shape),
        out_shape=jax.ShapeDtypeStruct(att_query.shape, jnp.bfloat16),
        scratch_shapes=[
            pltpu.VMEM((size, DIM), jnp.bfloat16),
            pltpu.VMEM((tokens, DIM), jnp.bfloat16),
            pltpu.VMEM((tokens, DIM), jnp.bfloat16),
            pltpu.VMEM((tokens // step, size, step), jnp.float32),
            pltpu.VMEM((size, DIM), jnp.float32),
            pltpu.VMEM((size, DIM), jnp.float32),
            pltpu.VMEM((size, DIM), jnp.float32),
        ],
        compiler_params=pltpu.CompilerParams(vmem_limit_bytes=48 * 1024 * 1024),
        cost_estimate=pl.CostEstimate(
            flops=4 * rows * HEADS * tokens * DIM, bytes_accessed=3 << 20, transcendentals=0
        ),
        name="causal",
    )(me, att_query, far, own)


def passed_along(block, axis):
    count = lax.axis_size(axis)
    return lax.ppermute(block, axis, [(i, i + 1) for i in range(count - 1)])


def per_device(tri_query, tri_keys, att_query, norm_gain, kv_weight):
    rows = tri_query.shape[0]
    half = rows // 2
    shards = lax.axis_size("seq")
    me = lax.axis_index("seq")
    place = jnp.reshape(me, (1,)).astype(jnp.int32)
    gain = norm_gain.reshape(1, -1)
    behind = passed_along(tri_keys, "seq")
    held, kv_late = tri_call(place, tri_query, behind, tri_keys, gain, kv_weight, None, 1, half)
    before = passed_along(kv_late[half - shards :], "seq")
    tri_out, kv_early = tri_call(place, tri_query, behind, tri_keys, gain, kv_weight, held, 0, half)
    own = jnp.concatenate([kv_early, kv_late], 0)
    share = lax.dynamic_slice_in_dim(jnp.concatenate([before, own], 0), shards - me, rows - 1, 0)
    far = lax.all_gather(share, "seq", axis=0, tiled=True)
    attended = att_call(place, att_query, far, own)
    return (tri_out, attended)


def solution(mesh):
    in_specs = (P(("dp", "seq"), None), P(("dp", "seq"), None), P(("dp", "seq"), None), P(), P())
    out_specs = (P(("dp", "seq"), None), P(("dp", "seq"), None))
    return jax.shard_map(
        per_device, mesh=mesh, in_specs=in_specs, out_specs=out_specs, check_vma=False
    )
```

time: 167 us -> 80 us (0.48)
  the two profiles are of different devices: /device:TPU:1 before, /device:TPU:481 now
where the time goes in v1:
time: 80 us; the launch traced here: 79.7 us
  Pallas kernels  48.9 us (61%)
  blocking collectives  20.9 us (26%)
  local copies, waits for them, and re-layouts  4.21 us (5%)
  starting transfers between devices  2.57 us (3%)
  waiting for transfers between devices  2.32 us (3%)
    pallas_call x2, Pallas kernels, tri_call(): pl.pallas_call(kernel, grid=(1,), in_specs=in_specs, out_specs=[pl.BlockS...  31.7 us
    all_gather x1, blocking collectives, per_device(): far = lax.all_gather(share, 'seq', axis=0, tiled=True)  20.9 us
    pallas_call x1, Pallas kernels, att_call(): pl.pallas_call(functools.partial(att_kernel, rows=rows, step=step, group=...  17.2 us
    unnamed x11, local copies, waits for them, and re-layouts  4.21 us
    ppermute x2, starting transfers between devices, passed_along(): return lax.ppermute(block, axis, [(i, i + 1) for i in range(count - 1)])  2.57 us
    ppermute x2, waiting for transfers between devices, passed_along(): return lax.ppermute(block, axis, [(i, i + 1) for i in range(count - 1)])  2.32 us
  transfers between devices with their start and end apart: 2, of which 1 were waited for; matrix products, arithmetic and copies ran while one was open for 0% of the time, Pallas kernels for 20%

profile of v1, /device:TPU:481, one launch (start us, length us, event | category | flops | bytes accessed | tf_op | source)
XLA Modules:
  0.0 79.7 jit_solution(13825455897153992746)
XLA Ops:
  0.6 1.3 %collective-permute-start = (bf16[128,512]{1,0:T(8,128)(2,1)}, bf16[128,512]{1,0:T(8,128)(2,1)S(1)}, u32[]{:S(2)}, u32[]{:S(2)}) collective-permute-start(bf16[128,512]{1,0:T(8,128)(2,1)} %cur_ref.1), channel_id=1, source_target_pairs={{0,1},{1,2},{2,3},{3,4},{4,5},{5,6},{6,7},{7,8},{8,9},{9,10},{10,1... | collective-permute-start | bytes 393224 | tf_op jit(solution)/shard_map/ppermute | solution.py:245
  1.9 0.0 copy-start.4
  1.9 2.3 %collective-permute-done.refs_2_.prev_ref = bf16[128,512]{1,0:T(8,128)(2,1)S(1)} collective-permute-done((bf16[128,512]{1,0:T(8,128)(2,1)}, bf16[128,512]{1,0:T(8,128)(2,1)S(1)}, u32[]{:S(2)}, u32[]{:S(2)}) %collective-permute-start) | collective-permute-done | bytes 131104 | tf_op jit(solution)/shard_map/ppermute | solution.py:245
  4.3 0.0 copy-done.4
  4.3 0.0 copy-start
  4.3 1.2 %copy-done = bf16[2048,256]{1,0:T(8,128)(2,1)S(1)} copy-done((bf16[2048,256]{1,0:T(8,128)(2,1)S(1)}, bf16[2048,256]{1,0:T(8,128)(2,1)}, u32[]{:S(2)}) %copy-start) | copy-done | bytes 1048600
  5.5 0.0 copy-start.1
  5.5 1.0 %copy-done.1 = bf16[128,2048]{1,0:T(8,128)(2,1)S(1)} copy-done((bf16[128,2048]{1,0:T(8,128)(2,1)S(1)}, bf16[128,2048]{1,0:T(8,128)(2,1)}, u32[]{:S(2)}) %copy-start.1) | copy-done | bytes 524312
  6.5 0.0 copy-start.3
  6.5 0.9 %copy-done.3 = bf16[128,512]{1,0:T(8,128)(2,1)S(1)} copy-done((bf16[128,512]{1,0:T(8,128)(2,1)S(1)}, bf16[128,512]{1,0:T(8,128)(2,1)}, u32[]{:S(2)}) %copy-start.3) | copy-done | bytes 131096
  7.4 15.8 %tri_part.2 = (bf16[128,2048]{1,0:T(8,128)(2,1)}, bf16[64,256]{1,0:T(8,128)(2,1)S(1)}) custom-call(s32[1]{0:T(128)} %bitcast.refs_0_.me_ref, bf16[128,2048]{1,0:T(8,128)(2,1)S(1)} %copy-done.1, bf16[128,512]{1,0:T(8,128)(2,1)S(1)} %collective-permute-done.refs_2_.prev_ref, bf16[128,512]{1,0:T(8,128)(2,1)S(1)} %copy-done.3, f32[1,2048]{1,0:T(1,128)S(1)} %bitcast.4, ...), custom_call_target="tpu_custom_call" | custom-call | flops 2147483648 | bytes 2097152 | tf_op jit(solution)/shard_map/tri_part/pallas_call | solution.py:107
  23.3 1.3 %collective-permute-start.1 = (bf16[16,256]{1,0:T(8,128)(2,1)S(1)}, bf16[16,256]{1,0:T(8,128)(2,1)S(1)}, u32[]{:S(2)}, u32[]{:S(2)}) collective-permute-start(bf16[16,256]{1,0:T(8,128)(2,1)S(1)} %slice.3), channel_id=1, source_target_pairs={{0,1},{1,2},{2,3},{3,4},{4,5},{5,6},{6,7},{7,8},{8,9},{9,10},{10,1... | collective-permute-start | bytes 24584 | tf_op jit(solution)/shard_map/ppermute | solution.py:245
  24.6 15.8 %tri_part.3 = (bf16[128,2048]{1,0:T(8,128)(2,1)}, bf16[64,256]{1,0:T(8,128)(2,1)S(1)}) custom-call(s32[1]{0:T(128)} %bitcast.refs_0_.me_ref, bf16[128,2048]{1,0:T(8,128)(2,1)S(1)} %copy-done.1, bf16[128,512]{1,0:T(8,128)(2,1)S(1)} %collective-permute-done.refs_2_.prev_ref, bf16[128,512]{1,0:T(8,128)(2,1)S(1)} %copy-done.3, ...), custom_call_target="tpu_custom_call", output_to_operand_aliasing={{0}: (6, {})} | custom-call | flops 2147483648 | bytes 2097152 | tf_op jit(solution)/shard_map/tri_part/pallas_call | solution.py:107
  40.4 0.0 collective-permute-done.1
  40.4 0.1 fusion.2
  40.5 20.9 %all-gather = bf16[16,127,256]{2,1,0:T(8,128)(2,1)S(1)} all-gather(bf16[1,127,256]{2,1,0:T(8,128)(2,1)S(1)} %fusion.2), channel_id=1, replica_groups=mesh['dp'=32,'seq'=16] {'seq'}, dimensions={0}, use_global_device_ids=true | all-gather | bytes 1105408 | tf_op jit(solution)/shard_map/all_gather | solution.py:261
  61.4 0.0 copy-start.2
  61.4 0.3 reshape.13.far_ref
  61.7 0.7 copy-done.2
  62.5 17.2 %causal.1 = bf16[128,2048]{1,0:T(8,128)(2,1)} custom-call(s32[1]{0:T(128)} %bitcast.refs_0_.me_ref, bf16[128,2048]{1,0:T(8,128)(2,1)S(1)} %copy-done.2, bf16[2032,256]{1,0:T(8,128)(2,1)S(1)} %reshape.13.far_ref, bf16[128,256]{1,0:T(8,128)(2,1)S(1)} %pad_maximum_fusion.own_ref), custom_call_target="tpu_custom_call" | custom-call | flops 2147483648 | bytes 3145728 | tf_op jit(solution)/shard_map/causal/pallas_call | solution.py:215
  (2 shorter events, 0.0 us)
Async XLA Ops:
  0.6 3.6 %collective-permute-start = (bf16[128,512]{1,0:T(8,128)(2,1)}, bf16[128,512]{1,0:T(8,128)(2,1)S(1)}, u32[]{:S(2)}, u32[]{:S(2)}) collective-permute-start(bf16[128,512]{1,0:T(8,128)(2,1)} %cur_ref.1), channel_id=1, source_target_pairs={{0,1},{1,2},{2,3},{3,4},{4,5},{5,6},{6,7},{7,8},{8,9},{9,10},{10,1... | collective-permute-start | bytes 393224 | tf_op jit(solution)/shard_map/ppermute | solution.py:245
  1.9 2.3 %copy-start.4 = (f32[2048]{0:T(1024)S(1)}, f32[2048]{0:T(1024)}, u32[]{:S(2)}) copy-start(f32[2048]{0:T(1024)} %param.8) | copy-start | bytes 24580
  4.3 1.2 %copy-start = (bf16[2048,256]{1,0:T(8,128)(2,1)S(1)}, bf16[2048,256]{1,0:T(8,128)(2,1)}, u32[]{:S(2)}) copy-start(bf16[2048,256]{1,0:T(8,128)(2,1)} %weight_ref.1) | copy-start | bytes 3145732
  5.5 1.0 %copy-start.1 = (bf16[128,2048]{1,0:T(8,128)(2,1)S(1)}, bf16[128,2048]{1,0:T(8,128)(2,1)}, u32[]{:S(2)}) copy-start(bf16[128,2048]{1,0:T(8,128)(2,1)} %q_ref.2) | copy-start | bytes 1572868
  6.5 0.9 %copy-start.3 = (bf16[128,512]{1,0:T(8,128)(2,1)S(1)}, bf16[128,512]{1,0:T(8,128)(2,1)}, u32[]{:S(2)}) copy-start(bf16[128,512]{1,0:T(8,128)(2,1)} %cur_ref.1) | copy-start | bytes 393220
  23.3 17.1 %collective-permute-start.1 = (bf16[16,256]{1,0:T(8,128)(2,1)S(1)}, bf16[16,256]{1,0:T(8,128)(2,1)S(1)}, u32[]{:S(2)}, u32[]{:S(2)}) collective-permute-start(bf16[16,256]{1,0:T(8,128)(2,1)S(1)} %slice.3), channel_id=1, source_target_pairs={{0,1},{1,2},{2,3},{3,4},{4,5},{5,6},{6,7},{7,8},{8,9},{9,10},{10,1... | collective-permute-start | bytes 24584 | tf_op jit(solution)/shard_map/ppermute | solution.py:245
  61.4 1.0 %copy-start.2 = (bf16[128,2048]{1,0:T(8,128)(2,1)S(1)}, bf16[128,2048]{1,0:T(8,128)(2,1)}, u32[]{:S(2)}) copy-start(bf16[128,2048]{1,0:T(8,128)(2,1)} %q_ref.3) | copy-start | bytes 1572868

commit v2 on v1

v2 whole, which is shorter than its diff:
```python
import functools

import jax
import jax.numpy as jnp
from jax import lax
from jax.experimental import pallas as pl
from jax.experimental.pallas import tpu as pltpu
from jax.sharding import PartitionSpec as P

HEADS = 16
DIM = 128
W1 = 128
W2 = 16
NEG = -1e30
SCALE = DIM**-0.5
EXP2_SCALE = SCALE * 1.4426950408889634
PIECE = 16
BLOCK = 16
NT = (((1,), (1,)), ((), ()))


def tri_kernel(
    me_ref, q_ref, prev_ref, cur_ref, gain_ref, weight_ref, held_ref, out_ref, kv_ref,
    k2_scr, v2_scr, mask_scr, s_scr, top_scr, square_scr, shift_scr, *, first_row, rows,
):
    first_shard = me_ref[0] == 0

    shift_scr[0:16, :] = prev_ref[W1 - 16 : W1, 2 * DIM :].astype(jnp.float32)
    shift_scr[16:, :] = cur_ref[:, 2 * DIM :].astype(jnp.float32)
    for lag in range(W2):
        at = 16 + first_row - lag
        k2_scr[lag] = shift_scr[at : at + rows, :DIM].astype(jnp.bfloat16)
        v2_scr[lag] = shift_scr[at : at + rows, DIM:]
    row = first_row + lax.broadcasted_iota(jnp.int32, (rows, DIM), 0)
    col = lax.broadcasted_iota(jnp.int32, (rows, DIM), 1)
    own = col <= row
    mask_scr[0] = jnp.where(own, 1.0, 0.0).astype(jnp.bfloat16)
    k1 = jnp.concatenate([cur_ref[:, :DIM], prev_ref[:, :DIM]], 0)
    v1 = jnp.concatenate([cur_ref[:, DIM : 2 * DIM], prev_ref[:, DIM : 2 * DIM]], 0)

    blocks = [slice(at, at + BLOCK) for at in range(0, rows, BLOCK)]
    pieces = [slice(at, at + PIECE) for at in range(0, W2, PIECE)]

    def lanes_of(head):
        return pl.ds(pl.multiple_of(head * DIM, DIM), DIM)

    def score_step(query, block, lags, slot, top, first):
        mq = jnp.concatenate([query * k2_scr[lag, block] for lag in range(lags.start, lags.stop)], 0)
        both = lax.dot_general(mq, k1, NT, preferred_element_type=jnp.float32)
        row = first_row + block.start + lax.broadcasted_iota(jnp.int32, (BLOCK, DIM), 0)
        own = lax.broadcasted_iota(jnp.int32, (BLOCK, DIM), 1) <= row
        for n, lag in enumerate(range(lags.start, lags.stop)):
            here = both[n * BLOCK : (n + 1) * BLOCK]
            if first:
                allowed = own
                if first_row + block.start < lag:
                    allowed = own & (lag <= row)
                score = jnp.where(allowed, here[:, :DIM], NEG)
            else:
                score = jnp.where(own, here[:, :DIM], here[:, DIM:])
            s_scr[slot, lag, block] = score
            top = score if top is None else jnp.maximum(top, score)
        return top

    def weigh_step(block, lags, slot, top, total, acc):
        halves = []
        mask = mask_scr[0, block]
        for lag in range(lags.start, lags.stop):
            weight = jnp.exp2((s_scr[slot, lag, block] - top) * EXP2_SCALE)
            total = weight if total is None else total + weight
            rounded = weight.astype(jnp.bfloat16)
            w_own = rounded * mask
            halves.append(jnp.concatenate([w_own, rounded - w_own], -1))
        paired = jnp.dot(jnp.concatenate(halves, 0), v1, preferred_element_type=jnp.float32)
        for n, lag in enumerate(range(lags.start, lags.stop)):
            part = paired[n * BLOCK : (n + 1) * BLOCK] * v2_scr[lag, block]
            acc = part if acc is None else acc + part
        return total, acc

    def spread(top):
        return jnp.broadcast_to(jnp.max(top, axis=-1, keepdims=True), top.shape)

    def both_steps(score_head, score_slot, weigh_head, first):
        for block in blocks:
            query = q_ref[block, lanes_of(score_head)]
            next_top = total = acc = None
            top = top_scr[1 - score_slot, block]
            for lags in pieces:
                next_top = score_step(query, block, lags, score_slot, next_top, first)
                total, acc = weigh_step(block, lags, 1 - score_slot, top, total, acc)
            top_scr[score_slot, block] = spread(next_top)
            result = (acc / jnp.sum(total, axis=-1, keepdims=True)).astype(jnp.bfloat16)
            out_ref[block, lanes_of(weigh_head)] = result
            wide = result.astype(jnp.float32)
            square_scr[block] += wide * wide

    def all_heads(first):
        square_scr[...] = jnp.zeros((rows, DIM), jnp.float32)
        for block in blocks:
            top = None
            for lags in pieces:
                top = score_step(q_ref[block, lanes_of(0)], block, lags, 0, top, first)
            top_scr[0, block] = spread(top)

        def pair(k, carried):
            both_steps(2 * k + 1, 1, 2 * k, first)
            both_steps(jnp.minimum(2 * k + 2, HEADS - 1), 0, 2 * k + 1, first)
            return carried

        lax.fori_loop(0, HEADS // 2, pair, 0)
        return square_scr[...]

    def finish(square):
        mean = jnp.sum(square, axis=-1, keepdims=True) * (1.0 / (HEADS * DIM))
        inverse = lax.rsqrt(mean + 1e-6)
        normed = (out_ref[...].astype(jnp.float32) * inverse * gain_ref[...]).astype(jnp.bfloat16)
        kv_ref[...] = jnp.dot(
            normed, weight_ref[...], preferred_element_type=jnp.float32
        ).astype(jnp.bfloat16)

    @pl.when(first_shard)
    def _():
        finish(all_heads(True))

    @pl.when(jnp.logical_not(first_shard))
    def _():
        finish(all_heads(False))


def tri_call(me, tri_query, behind, tri_keys, gain, kv_weight, held, number, rows):
    token_rows, width = tri_query.shape
    whole = lambda shape: pl.BlockSpec(shape, lambda i: (0,) * len(shape))
    in_specs = [
        pl.BlockSpec(memory_space=pltpu.SMEM),
        pl.BlockSpec((rows, width), lambda i: (number, 0)),
        whole(behind.shape),
        whole(tri_keys.shape),
        whole(gain.shape),
        whole(kv_weight.shape),
    ]
    args = [me, tri_query, behind, tri_keys, gain, kv_weight]
    body = functools.partial(tri_kernel, first_row=number * rows, rows=rows)
    aliases = {}
    if held is None:
        kernel = lambda *refs: body(*refs[:6], None, *refs[6:])
    else:
        kernel = body
        in_specs.append(pl.BlockSpec(memory_space=pl.ANY))
        args.append(held)
        aliases = {6: 0}
    return pl.pallas_call(
        kernel,
        grid=(1,),
        in_specs=in_specs,
        out_specs=[
            pl.BlockSpec((rows, width), lambda i: (number, 0)),
            whole((rows, 2 * DIM)),
        ],
        out_shape=[
            jax.ShapeDtypeStruct((token_rows, width), jnp.bfloat16),
            jax.ShapeDtypeStruct((rows, 2 * DIM), jnp.bfloat16),
        ],
        scratch_shapes=[
            pltpu.VMEM((W2, rows, DIM), jnp.bfloat16),
            pltpu.VMEM((W2, rows, DIM), jnp.float32),
            pltpu.VMEM((1, rows, DIM), jnp.bfloat16),
            pltpu.VMEM((2, W2, rows, DIM), jnp.float32),
            pltpu.VMEM((2, rows, DIM), jnp.float32),
            pltpu.VMEM((rows, DIM), jnp.float32),
            pltpu.VMEM((W1 + 16, 2 * DIM), jnp.float32),
        ],
        input_output_aliases=aliases,
        compiler_params=pltpu.CompilerParams(vmem_limit_bytes=40 * 1024 * 1024),
        cost_estimate=pl.CostEstimate(
            flops=4 * rows * HEADS * W2 * 256 * DIM, bytes_accessed=2 << 20, transcendentals=0
        ),
        name="tri_part",
    )(*args)


KEYS = 256


def att_kernel(me_ref, q_ref, far_ref, own_ref, out_ref, k_scr, v_scr, s_scr, top_scr, *, rows):
    me = me_ref[0]
    tokens = k_scr.shape[0]
    before = tokens - rows
    k_scr[:before, :] = far_ref[:before, :DIM]
    v_scr[:before, :] = far_ref[:before, DIM:]
    k_scr[before:, :] = own_ref[:, :DIM]
    v_scr[before:, :] = own_ref[:, DIM:]
    tiles = tokens // DIM
    caps = [jnp.where(tile < me, -NEG, NEG) for tile in range(tiles - 1)]

    def lanes_of(head):
        return pl.ds(pl.multiple_of(head * DIM, DIM), DIM)

    def score_step(query, slot, at, top):
        both = lax.dot_general(
            query, k_scr[at : at + KEYS, :], NT, preferred_element_type=jnp.float32
        )
        for n in range(KEYS // DIM):
            tile = at // DIM + n
            score = both[:, n * DIM : (n + 1) * DIM]
            if tile == tiles - 1:
                row = lax.broadcasted_iota(jnp.int32, (rows, DIM), 0)
                col = lax.broadcasted_iota(jnp.int32, (rows, DIM), 1)
                score = jnp.where(col <= row, score, NEG)
            else:
                score = jnp.minimum(score, caps[tile])
            s_scr[slot, tile] = score
            top = score if top is None else jnp.maximum(top, score)
        return top

    def weigh_step(slot, at, top, total, acc):
        weights = []
        for n in range(KEYS // DIM):
            weight = jnp.exp2((s_scr[slot, at // DIM + n] - top) * EXP2_SCALE)
            total = weight if total is None else total + weight
            weights.append(weight.astype(jnp.bfloat16))
        return total, (acc or []) + weights

    def settle(slot, top):
        top_scr[slot] = jnp.broadcast_to(jnp.max(top, axis=-1, keepdims=True), (rows, DIM))

    def both_steps(score_head, score_slot, weigh_head):
        query = q_ref[:, lanes_of(score_head)]
        next_top = total = acc = None
        top = top_scr[1 - score_slot]
        for at in range(0, tokens, KEYS):
            next_top = score_step(query, score_slot, at, next_top)
            total, acc = weigh_step(1 - score_slot, at, top, total, acc)
        settle(score_slot, next_top)
        acc = jnp.dot(jnp.concatenate(acc, -1), v_scr[...], preferred_element_type=jnp.float32)
        result = acc / jnp.sum(total, axis=-1, keepdims=True)
        out_ref[:, lanes_of(weigh_head)] = result.astype(jnp.bfloat16)

    top = None
    for at in range(0, tokens, KEYS):
        top = score_step(q_ref[:, lanes_of(0)], 0, at, top)
    settle(0, top)

    def pair(k, carried):
        both_steps(2 * k + 1, 1, 2 * k)
        both_steps(jnp.minimum(2 * k + 2, HEADS - 1), 0, 2 * k + 1)
        return carried

    lax.fori_loop(0, HEADS // 2, pair, 0)


def att_call(me, att_query, far, own):
    rows, width = att_query.shape
    tokens = 16 * rows
    whole = lambda shape: pl.BlockSpec(shape, lambda i: (0,) * len(shape))
    return pl.pallas_call(
        functools.partial(att_kernel, rows=rows),
        grid=(1,),
        in_specs=[
            pl.BlockSpec(memory_space=pltpu.SMEM),
            whole(att_query.shape),
            whole(far.shape),
            whole(own.shape),
        ],
        out_specs=whole(att_query.shape),
        out_shape=jax.ShapeDtypeStruct(att_query.shape, jnp.bfloat16),
        scratch_shapes=[
            pltpu.VMEM((tokens, DIM), jnp.bfloat16),
            pltpu.VMEM((tokens, DIM), jnp.bfloat16),
            pltpu.VMEM((2, tokens // DIM, rows, DIM), jnp.float32),
            pltpu.VMEM((2, rows, DIM), jnp.float32),
        ],
        compiler_params=pltpu.CompilerParams(vmem_limit_bytes=48 * 1024 * 1024),
        cost_estimate=pl.CostEstimate(
            flops=4 * rows * HEADS * tokens * DIM, bytes_accessed=3 << 20, transcendentals=0
        ),
        name="causal",
    )(me, att_query, far, own)


def passed_along(block, axis):
    count = lax.axis_size(axis)
    return lax.ppermute(block, axis, [(i, i + 1) for i in range(count - 1)])


def per_device(tri_query, tri_keys, att_query, norm_gain, kv_weight):
    rows = tri_query.shape[0]
    half = rows // 2
    shards = lax.axis_size("seq")
    me = lax.axis_index("seq")
    place = jnp.reshape(me, (1,)).astype(jnp.int32)
    gain = norm_gain.reshape(1, -1)
    behind = passed_along(tri_keys, "seq")
    held, kv_late = tri_call(place, tri_query, behind, tri_keys, gain, kv_weight, None, 1, half)
    before = passed_along(kv_late[half - shards :], "seq")
    tri_out, kv_early = tri_call(place, tri_query, behind, tri_keys, gain, kv_weight, held, 0, half)
    own = jnp.concatenate([kv_early, kv_late], 0)
    share = lax.dynamic_slice_in_dim(jnp.concatenate([before, own], 0), shards - me, rows - 1, 0)
    far = lax.all_gather(share, "seq", axis=0, tiled=True)
    attended = att_call(place, att_query, far, own)
    return (tri_out, attended)


def solution(mesh):
    in_specs = (P(("dp", "seq"), None), P(("dp", "seq"), None), P(("dp", "seq"), None), P(), P())
    out_specs = (P(("dp", "seq"), None), P(("dp", "seq"), None))
    return jax.shard_map(
        per_device, mesh=mesh, in_specs=in_specs, out_specs=out_specs, check_vma=False
    )
```

time: 80 us -> 65.2 us (0.82)
  the two profiles are of different devices: /device:TPU:481 before, /device:TPU:1 now
where the time goes in v2:
time: 65.2 us; the launch traced here: 64.9 us
  Pallas kernels  24.1 us (37%)
  blocking collectives  23.9 us (37%)
  starting transfers between devices  8.06 us (12%)
  local copies, waits for them, and re-layouts  4.21 us (6%)
  waiting for transfers between devices  3.8 us (6%)
  between operations  0.68 us (1%)
    all_gather x1, blocking collectives, per_device(): far = lax.all_gather(share, 'seq', axis=0, tiled=True)  23.9 us
    pallas_call x2, Pallas kernels, tri_call(): pl.pallas_call(kernel, grid=(1,), in_specs=in_specs, out_specs=[pl.BlockS...  15.4 us
    pallas_call x1, Pallas kernels, att_call(): pl.pallas_call(functools.partial(att_kernel, rows=rows), grid=(1,), in_sp...  8.67 us
    ppermute x2, starting transfers between devices, passed_along(): return lax.ppermute(block, axis, [(i, i + 1) for i in range(count - 1)])  8.06 us
    unnamed x11, local copies, waits for them, and re-layouts  4.21 us
    ppermute x2, waiting for transfers between devices, passed_along(): return lax.ppermute(block, axis, [(i, i + 1) for i in range(count - 1)])  3.8 us
  transfers between devices with their start and end apart: 2, of which 1 were waited for; matrix products, arithmetic and copies ran while one was open for 0% of the time, Pallas kernels for 12%

profile of v2, /device:TPU:1, one launch (start us, length us, event | category | flops | bytes accessed | tf_op | source)
XLA Modules:
  0.0 64.9 jit_solution(62580514728513266)
XLA Ops:
  0.6 5.4 %collective-permute-start = (bf16[128,512]{1,0:T(8,128)(2,1)}, bf16[128,512]{1,0:T(8,128)(2,1)S(1)}, u32[]{:S(2)}, u32[]{:S(2)}) collective-permute-start(bf16[128,512]{1,0:T(8,128)(2,1)} %cur_ref.1), channel_id=1, source_target_pairs={{0,1},{1,2},{2,3},{3,4},{4,5},{5,6},{6,7},{7,8},{8,9},{9,10},{10,1... | collective-permute-start | bytes 393224 | tf_op jit(solution)/shard_map/ppermute | solution.py:282
  6.0 0.0 copy-start.4
  6.0 3.8 %collective-permute-done.refs_2_.prev_ref = bf16[128,512]{1,0:T(8,128)(2,1)S(1)} collective-permute-done((bf16[128,512]{1,0:T(8,128)(2,1)}, bf16[128,512]{1,0:T(8,128)(2,1)S(1)}, u32[]{:S(2)}, u32[]{:S(2)}) %collective-permute-start) | collective-permute-done | bytes 131104 | tf_op jit(solution)/shard_map/ppermute | solution.py:282
  9.8 0.0 copy-done.4
  9.8 0.0 copy-start
  9.8 1.2 %copy-done = bf16[2048,256]{1,0:T(8,128)(2,1)S(1)} copy-done((bf16[2048,256]{1,0:T(8,128)(2,1)S(1)}, bf16[2048,256]{1,0:T(8,128)(2,1)}, u32[]{:S(2)}) %copy-start) | copy-done | bytes 1048600
  11.1 0.0 copy-start.1
  11.1 1.0 %copy-done.1 = bf16[128,2048]{1,0:T(8,128)(2,1)S(1)} copy-done((bf16[128,2048]{1,0:T(8,128)(2,1)S(1)}, bf16[128,2048]{1,0:T(8,128)(2,1)}, u32[]{:S(2)}) %copy-start.1) | copy-done | bytes 524312
  12.1 0.0 copy-start.3
  12.1 0.9 %copy-done.3 = bf16[128,512]{1,0:T(8,128)(2,1)S(1)} copy-done((bf16[128,512]{1,0:T(8,128)(2,1)S(1)}, bf16[128,512]{1,0:T(8,128)(2,1)}, u32[]{:S(2)}) %copy-start.3) | copy-done | bytes 131096
  13.0 7.7 %tri_part.2 = (bf16[128,2048]{1,0:T(8,128)(2,1)}, bf16[64,256]{1,0:T(8,128)(2,1)S(1)}) custom-call(s32[1]{0:T(128)} %bitcast.refs_0_.me_ref, bf16[128,2048]{1,0:T(8,128)(2,1)S(1)} %copy-done.1, bf16[128,512]{1,0:T(8,128)(2,1)S(1)} %collective-permute-done.refs_2_.prev_ref, bf16[128,512]{1,0:T(8,128)(2,1)S(1)} %copy-done.3, f32[1,2048]{1,0:T(1,128)S(1)} %bitcast.4, ...), custom_call_target="tpu_custom_call" | custom-call | flops 2147483648 | bytes 2097152 | tf_op jit(solution)/shard_map/tri_part/pallas_call | solution.py:151
  20.7 2.7 %collective-permute-start.1 = (bf16[16,256]{1,0:T(8,128)(2,1)S(1)}, bf16[16,256]{1,0:T(8,128)(2,1)S(1)}, u32[]{:S(2)}, u32[]{:S(2)}) collective-permute-start(bf16[16,256]{1,0:T(8,128)(2,1)S(1)} %slice.3), channel_id=1, source_target_pairs={{0,1},{1,2},{2,3},{3,4},{4,5},{5,6},{6,7},{7,8},{8,9},{9,10},{10,1... | collective-permute-start | bytes 24584 | tf_op jit(solution)/shard_map/ppermute | solution.py:282
  23.4 7.7 %tri_part.3 = (bf16[128,2048]{1,0:T(8,128)(2,1)}, bf16[64,256]{1,0:T(8,128)(2,1)S(1)}) custom-call(s32[1]{0:T(128)} %bitcast.refs_0_.me_ref, bf16[128,2048]{1,0:T(8,128)(2,1)S(1)} %copy-done.1, bf16[128,512]{1,0:T(8,128)(2,1)S(1)} %collective-permute-done.refs_2_.prev_ref, bf16[128,512]{1,0:T(8,128)(2,1)S(1)} %copy-done.3, ...), custom_call_target="tpu_custom_call", output_to_operand_aliasing={{0}: (6, {})} | custom-call | flops 2147483648 | bytes 2097152 | tf_op jit(solution)/shard_map/tri_part/pallas_call | solution.py:151
  31.1 0.0 collective-permute-done.1
  31.1 0.1 fusion.2
  31.3 23.9 %all-gather = bf16[16,127,256]{2,1,0:T(8,128)(2,1)S(1)} all-gather(bf16[1,127,256]{2,1,0:T(8,128)(2,1)S(1)} %fusion.2), channel_id=1, replica_groups=mesh['dp'=32,'seq'=16] {'seq'}, dimensions={0}, use_global_device_ids=true | all-gather | bytes 1105408 | tf_op jit(solution)/shard_map/all_gather | solution.py:298
  55.2 0.0 copy-start.2
  55.2 0.3 reshape.13.far_ref
  55.5 0.7 %copy-done.2 = bf16[128,2048]{1,0:T(8,128)(2,1)S(1)} copy-done((bf16[128,2048]{1,0:T(8,128)(2,1)S(1)}, bf16[128,2048]{1,0:T(8,128)(2,1)}, u32[]{:S(2)}) %copy-start.2) | copy-done | bytes 524312
  56.2 8.7 %causal.1 = bf16[128,2048]{1,0:T(8,128)(2,1)} custom-call(s32[1]{0:T(128)} %bitcast.refs_0_.me_ref, bf16[128,2048]{1,0:T(8,128)(2,1)S(1)} %copy-done.2, bf16[2032,256]{1,0:T(8,128)(2,1)S(1)} %reshape.13.far_ref, bf16[128,256]{1,0:T(8,128)(2,1)S(1)} %pad_maximum_fusion.own_ref), custom_call_target="tpu_custom_call" | custom-call | flops 2147483648 | bytes 3145728 | tf_op jit(solution)/shard_map/causal/pallas_call | solution.py:255
  (2 shorter events, 0.0 us)
Async XLA Ops:
  0.6 9.2 %collective-permute-start = (bf16[128,512]{1,0:T(8,128)(2,1)}, bf16[128,512]{1,0:T(8,128)(2,1)S(1)}, u32[]{:S(2)}, u32[]{:S(2)}) collective-permute-start(bf16[128,512]{1,0:T(8,128)(2,1)} %cur_ref.1), channel_id=1, source_target_pairs={{0,1},{1,2},{2,3},{3,4},{4,5},{5,6},{6,7},{7,8},{8,9},{9,10},{10,1... | collective-permute-start | bytes 393224 | tf_op jit(solution)/shard_map/ppermute | solution.py:282
  6.0 3.8 %copy-start.4 = (f32[2048]{0:T(1024)S(1)}, f32[2048]{0:T(1024)}, u32[]{:S(2)}) copy-start(f32[2048]{0:T(1024)} %param.8) | copy-start | bytes 24580
  9.8 1.2 %copy-start = (bf16[2048,256]{1,0:T(8,128)(2,1)S(1)}, bf16[2048,256]{1,0:T(8,128)(2,1)}, u32[]{:S(2)}) copy-start(bf16[2048,256]{1,0:T(8,128)(2,1)} %weight_ref.1) | copy-start | bytes 3145732
  11.1 1.0 %copy-start.1 = (bf16[128,2048]{1,0:T(8,128)(2,1)S(1)}, bf16[128,2048]{1,0:T(8,128)(2,1)}, u32[]{:S(2)}) copy-start(bf16[128,2048]{1,0:T(8,128)(2,1)} %q_ref.2) | copy-start | bytes 1572868
  12.1 0.9 %copy-start.3 = (bf16[128,512]{1,0:T(8,128)(2,1)S(1)}, bf16[128,512]{1,0:T(8,128)(2,1)}, u32[]{:S(2)}) copy-start(bf16[128,512]{1,0:T(8,128)(2,1)} %cur_ref.1) | copy-start | bytes 393220
  20.7 10.4 %collective-permute-start.1 = (bf16[16,256]{1,0:T(8,128)(2,1)S(1)}, bf16[16,256]{1,0:T(8,128)(2,1)S(1)}, u32[]{:S(2)}, u32[]{:S(2)}) collective-permute-start(bf16[16,256]{1,0:T(8,128)(2,1)S(1)} %slice.3), channel_id=1, source_target_pairs={{0,1},{1,2},{2,3},{3,4},{4,5},{5,6},{6,7},{7,8},{8,9},{9,10},{10,1... | collective-permute-start | bytes 24584 | tf_op jit(solution)/shard_map/ppermute | solution.py:282
  55.2 1.0 %copy-start.2 = (bf16[128,2048]{1,0:T(8,128)(2,1)S(1)}, bf16[128,2048]{1,0:T(8,128)(2,1)}, u32[]{:S(2)}) copy-start(bf16[128,2048]{1,0:T(8,128)(2,1)} %q_ref.3) | copy-start | bytes 1572868

commit v3 on v2

--- a/solution.py
+++ b/solution.py
@@ -20,7 +20,7 @@
 
 
 def tri_kernel(
-    me_ref, q_ref, prev_ref, cur_ref, gain_ref, weight_ref, held_ref, out_ref, kv_ref,
+    me_ref, staged_ref, q_ref, prev_ref, cur_ref, gain_ref, weight_ref, held_ref, out_ref, kv_ref,
     k2_scr, v2_scr, mask_scr, s_scr, top_scr, square_scr, shift_scr, *, first_row, rows,
 ):
     first_shard = me_ref[0] == 0
@@ -127,27 +127,28 @@
         finish(all_heads(False))
 
 
-def tri_call(me, tri_query, behind, tri_keys, gain, kv_weight, held, number, rows):
+def tri_call(me, staged, tri_query, behind, tri_keys, gain, kv_weight, held, number, rows):
     token_rows, width = tri_query.shape
     whole = lambda shape: pl.BlockSpec(shape, lambda i: (0,) * len(shape))
     in_specs = [
         pl.BlockSpec(memory_space=pltpu.SMEM),
+        pl.BlockSpec(memory_space=pl.ANY),
         pl.BlockSpec((rows, width), lambda i: (number, 0)),
         whole(behind.shape),
         whole(tri_keys.shape),
         whole(gain.shape),
         whole(kv_weight.shape),
     ]
-    args = [me, tri_query, behind, tri_keys, gain, kv_weight]
+    args = [me, staged, tri_query, behind, tri_keys, gain, kv_weight]
     body = functools.partial(tri_kernel, first_row=number * rows, rows=rows)
     aliases = {}
     if held is None:
-        kernel = lambda *refs: body(*refs[:6], None, *refs[6:])
+        kernel = lambda *refs: body(*refs[:7], None, *refs[7:])
     else:
         kernel = body
         in_specs.append(pl.BlockSpec(memory_space=pl.ANY))
         args.append(held)
-        aliases = {6: 0}
+        aliases = {7: 0}
     return pl.pallas_call(
         kernel,
         grid=(1,),
@@ -178,74 +179,106 @@
     )(*args)
 
 
-KEYS = 256
-
-
-def att_kernel(me_ref, q_ref, far_ref, own_ref, out_ref, k_scr, v_scr, s_scr, top_scr, *, rows):
+def stage_kernel(*refs):
+    out_ref = refs[-1]
+    total = jnp.zeros(out_ref.shape, jnp.float32)
+    for ref in refs[:-1]:
+        total += ref[0:1, 0:DIM].astype(jnp.float32)
+    out_ref[...] = total
+
+
+def stage_call(*arrays):
+    return pl.pallas_call(
+        stage_kernel,
+        grid=(1,),
+        in_specs=[pl.BlockSpec(a.shape, lambda i: (0, 0)) for a in arrays],
+        out_specs=pl.BlockSpec((8, DIM), lambda i: (0, 0)),
+        out_shape=jax.ShapeDtypeStruct((8, DIM), jnp.float32),
+        compiler_params=pltpu.CompilerParams(vmem_limit_bytes=8 * 1024 * 1024),
+        cost_estimate=pl.CostEstimate(flops=0, bytes_accessed=3 << 20, transcendentals=0),
+        name="stage",
+    )(*arrays)
+
+
+SPAN = 2
+
+
+def att_kernel(me_ref, q_ref, far_ref, own_ref, out_ref, s_scr, top_scr, *, rows):
     me = me_ref[0]
-    tokens = k_scr.shape[0]
-    before = tokens - rows
-    k_scr[:before, :] = far_ref[:before, :DIM]
-    v_scr[:before, :] = far_ref[:before, DIM:]
-    k_scr[before:, :] = own_ref[:, :DIM]
-    v_scr[before:, :] = own_ref[:, DIM:]
-    tiles = tokens // DIM
-    caps = [jnp.where(tile < me, -NEG, NEG) for tile in range(tiles - 1)]
+    shards = far_ref.shape[0] // rows + 1
 
     def lanes_of(head):
         return pl.ds(pl.multiple_of(head * DIM, DIM), DIM)
 
-    def score_step(query, slot, at, top):
-        both = lax.dot_general(
-            query, k_scr[at : at + KEYS, :], NT, preferred_element_type=jnp.float32
-        )
-        for n in range(KEYS // DIM):
-            tile = at // DIM + n
-            score = both[:, n * DIM : (n + 1) * DIM]
-            if tile == tiles - 1:
-                row = lax.broadcasted_iota(jnp.int32, (rows, DIM), 0)
-                col = lax.broadcasted_iota(jnp.int32, (rows, DIM), 1)
-                score = jnp.where(col <= row, score, NEG)
-            else:
-                score = jnp.minimum(score, caps[tile])
-            s_scr[slot, tile] = score
-            top = score if top is None else jnp.maximum(top, score)
-        return top
-
-    def weigh_step(slot, at, top, total, acc):
-        weights = []
-        for n in range(KEYS // DIM):
-            weight = jnp.exp2((s_scr[slot, at // DIM + n] - top) * EXP2_SCALE)
-            total = weight if total is None else total + weight
-            weights.append(weight.astype(jnp.bfloat16))
-        return total, (acc or []) + weights
-
-    def settle(slot, top):
-        top_scr[slot] = jnp.broadcast_to(jnp.max(top, axis=-1, keepdims=True), (rows, DIM))
-
-    def both_steps(score_head, score_slot, weigh_head):
-        query = q_ref[:, lanes_of(score_head)]
-        next_top = total = acc = None
-        top = top_scr[1 - score_slot]
-        for at in range(0, tokens, KEYS):
-            next_top = score_step(query, score_slot, at, next_top)
-            total, acc = weigh_step(1 - score_slot, at, top, total, acc)
-        settle(score_slot, next_top)
-        acc = jnp.dot(jnp.concatenate(acc, -1), v_scr[...], preferred_element_type=jnp.float32)
-        result = acc / jnp.sum(total, axis=-1, keepdims=True)
-        out_ref[:, lanes_of(weigh_head)] = result.astype(jnp.bfloat16)
-
-    top = None
-    for at in range(0, tokens, KEYS):
-        top = score_step(q_ref[:, lanes_of(0)], 0, at, top)
-    settle(0, top)
-
-    def pair(k, carried):
-        both_steps(2 * k + 1, 1, 2 * k)
-        both_steps(jnp.minimum(2 * k + 2, HEADS - 1), 0, 2 * k + 1)
-        return carried
-
-    lax.fori_loop(0, HEADS // 2, pair, 0)
+    def attend(before):
+        tiles = before + 1
+        caps = [jnp.where(tile < me, -NEG, NEG) for tile in range(before)]
+
+        def of_tile(tile, lanes):
+            if tile == before:
+                return own_ref[:, lanes]
+            return far_ref[tile * DIM : (tile + 1) * DIM, lanes]
+
+        def score_step(query, slot, tile, top):
+            keys = [of_tile(tile, slice(0, DIM)), of_tile(tile + 1, slice(0, DIM))]
+            both = lax.dot_general(
+                query, jnp.concatenate(keys, 0), NT, preferred_element_type=jnp.float32
+            )
+            for n in range(2):
+                score = both[:, n * DIM : (n + 1) * DIM]
+                if tile + n == before:
+                    row = lax.broadcasted_iota(jnp.int32, (rows, DIM), 0)
+                    col = lax.broadcasted_iota(jnp.int32, (rows, DIM), 1)
+                    score = jnp.where(col <= row, score, NEG)
+                else:
+                    score = jnp.minimum(score, caps[tile + n])
+                s_scr[slot, tile + n] = score
+                top = score if top is None else jnp.maximum(top, score)
+            return top
+
+        def weigh_step(slot, tile, top, total, weights):
+            for n in range(2):
+                weight = jnp.exp2((s_scr[slot, tile + n] - top) * EXP2_SCALE)
+                total = weight if total is None else total + weight
+                weights.append(weight.astype(jnp.bfloat16))
+            return total
+
+        def settle(slot, top):
+            top_scr[slot] = jnp.broadcast_to(jnp.max(top, axis=-1, keepdims=True), (rows, DIM))
+
+        def both_steps(score_head, score_slot, weigh_head):
+            query = q_ref[:, lanes_of(score_head)]
+            next_top = total = None
+            weights = []
+            top = top_scr[1 - score_slot]
+            for tile in range(0, tiles, 2):
+                next_top = score_step(query, score_slot, tile, next_top)
+                total = weigh_step(1 - score_slot, tile, top, total, weights)
+            settle(score_slot, next_top)
+            values = jnp.concatenate([of_tile(t, slice(DIM, 2 * DIM)) for t in range(tiles)], 0)
+            acc = jnp.dot(
+                jnp.concatenate(weights, -1), values, preferred_element_type=jnp.float32
+            )
+            result = acc / jnp.sum(total, axis=-1, keepdims=True)
+            out_ref[:, lanes_of(weigh_head)] = result.astype(jnp.bfloat16)
+
+        top = None
+        for tile in range(0, tiles, 2):
+            top = score_step(q_ref[:, lanes_of(0)], 0, tile, top)
+        settle(0, top)
+
+        def pair(k, carried):
+            both_steps(2 * k + 1, 1, 2 * k)
+            both_steps(jnp.minimum(2 * k + 2, HEADS - 1), 0, 2 * k + 1)
+            return carried
+
+        lax.fori_loop(0, HEADS // 2, pair, 0)
+
+    lowest = 0
+    for before in range(1, shards + 1, SPAN):
+        chosen = (me >= lowest) & (me <= before)
+        pl.when(chosen)(functools.partial(attend, before))
+        lowest = before + 1
 
 
 def att_call(me, att_query, far, own):
@@ -264,8 +297,6 @@
         out_specs=whole(att_query.shape),
         out_shape=jax.ShapeDtypeStruct(att_query.shape, jnp.bfloat16),
         scratch_shapes=[
-            pltpu.VMEM((tokens, DIM), jnp.bfloat16),
-            pltpu.VMEM((tokens, DIM), jnp.bfloat16),
             pltpu.VMEM((2, tokens // DIM, rows, DIM), jnp.float32),
             pltpu.VMEM((2, rows, DIM), jnp.float32),
         ],
@@ -290,9 +321,10 @@
     place = jnp.reshape(me, (1,)).astype(jnp.int32)
     gain = norm_gain.reshape(1, -1)
     behind = passed_along(tri_keys, "seq")
-    held, kv_late = tri_call(place, tri_query, behind, tri_keys, gain, kv_weight, None, 1, half)
+    staged = stage_call(tri_query, tri_keys, kv_weight)
+    held, kv_late = tri_call(place, staged, tri_query, behind, tri_keys, gain, kv_weight, None, 1, half)
     before = passed_along(kv_late[half - shards :], "seq")
-    tri_out, kv_early = tri_call(place, tri_query, behind, tri_keys, gain, kv_weight, held, 0, half)
+    tri_out, kv_early = tri_call(place, staged, tri_query, behind, tri_keys, gain, kv_weight, held, 0, half)
     own = jnp.concatenate([kv_early, kv_late], 0)
     share = lax.dynamic_slice_in_dim(jnp.concatenate([before, own], 0), shards - me, rows - 1, 0)
     far = lax.all_gather(share, "seq", axis=0, tiled=True)

time: 65.2 us -> 58.4 us (0.90)
  Pallas kernels: 24.1 us -> 19.7 us
  waiting for transfers between devices: 3.8 us -> 0.62 us
  local copies, waits for them, and re-layouts: 4.21 us -> 5.65 us
  starting transfers between devices: 8.06 us -> 7.32 us
    pallas_call x1, Pallas kernels: 8.67 us -> 4.26 us  [att_call(): pl.pallas_call(functools.partial(att_kernel, rows=rows), grid=(1,), in_sp...]
    ppermute x2, waiting for transfers between devices: 3.8 us -> 0.62 us  [passed_along(): return lax.ppermute(block, axis, [(i, i + 1) for i in range(count - 1)])]
    unnamed x11 -> x17, local copies, waits for them, and re-layouts: 4.21 us -> 5.65 us
    ppermute x2, starting transfers between devices: 8.06 us -> 7.32 us  [passed_along(): return lax.ppermute(block, axis, [(i, i + 1) for i in range(count - 1)])]
  transfers between devices with their start and end apart: 2 -> 2, of which waited for: 1 -> 1; matrix products, arithmetic and copies ran while one was open for 0% -> 0% of each run, Pallas kernels for 12% -> 13%
where the time goes in v3:
time: 58.4 us; the launch traced here: 58 us
  blocking collectives  23.9 us (41%)
  Pallas kernels  19.7 us (34%)
  starting transfers between devices  7.32 us (13%)
  local copies, waits for them, and re-layouts  5.65 us (10%)
  between operations  0.68 us (1%)
  waiting for transfers between devices  0.62 us (1%)
    all_gather x1, blocking collectives, per_device(): far = lax.all_gather(share, 'seq', axis=0, tiled=True)  23.9 us
    pallas_call x2, Pallas kernels, tri_call(): pl.pallas_call(kernel, grid=(1,), in_specs=in_specs, out_specs=[pl.BlockS...  15.4 us
    ppermute x2, starting transfers between devices, passed_along(): return lax.ppermute(block, axis, [(i, i + 1) for i in range(count - 1)])  7.32 us
    unnamed x17, local copies, waits for them, and re-layouts  5.65 us
    pallas_call x1, Pallas kernels, att_call(): pl.pallas_call(functools.partial(att_kernel, rows=rows), grid=(1,), in_sp...  4.26 us
  transfers between devices with their start and end apart: 2, of which 1 were waited for; matrix products, arithmetic and copies ran while one was open for 0% of the time, Pallas kernels for 13%

profile of v3, /device:TPU:1, one launch (start us, length us, event | category | flops | bytes accessed | tf_op | source)
XLA Modules:
  0.0 58.0 jit_solution(1208483528393399798)
XLA Ops:
  0.6 5.4 %collective-permute-start = (bf16[128,512]{1,0:T(8,128)(2,1)}, bf16[128,512]{1,0:T(8,128)(2,1)S(1)}, u32[]{:S(2)}, u32[]{:S(2)}) collective-permute-start(bf16[128,512]{1,0:T(8,128)(2,1)} %cur_ref.1), channel_id=1, source_target_pairs={{0,1},{1,2},{2,3},{3,4},{4,5},{5,6},{6,7},{7,8},{8,9},{9,10},{10,1... | collective-permute-start | bytes 393224 | tf_op jit(solution)/shard_map/ppermute | solution.py:313
  6.0 0.0 copy-start
  6.0 1.2 %copy-done = bf16[2048,256]{1,0:T(8,128)(2,1)S(1)} copy-done((bf16[2048,256]{1,0:T(8,128)(2,1)S(1)}, bf16[2048,256]{1,0:T(8,128)(2,1)}, u32[]{:S(2)}) %copy-start) | copy-done | bytes 1048600
  7.3 0.0 copy-start.2
  7.3 1.0 %copy-done.2 = bf16[128,2048]{1,0:T(8,128)(2,1)S(1)} copy-done((bf16[128,2048]{1,0:T(8,128)(2,1)S(1)}, bf16[128,2048]{1,0:T(8,128)(2,1)}, u32[]{:S(2)}) %copy-start.2) | copy-done | bytes 524312
  8.3 0.0 copy-start.4
  8.3 0.9 %copy-done.4 = bf16[128,512]{1,0:T(8,128)(2,1)S(1)} copy-done((bf16[128,512]{1,0:T(8,128)(2,1)S(1)}, bf16[128,512]{1,0:T(8,128)(2,1)}, u32[]{:S(2)}) %copy-start.4) | copy-done | bytes 131096
  9.2 0.0 copy-start.1
  9.2 0.0 copy-start.3
  9.2 0.0 copy-start.5
  9.2 0.6 %collective-permute-done.refs_3_.prev_ref = bf16[128,512]{1,0:T(8,128)(2,1)S(1)} collective-permute-done((bf16[128,512]{1,0:T(8,128)(2,1)}, bf16[128,512]{1,0:T(8,128)(2,1)S(1)}, u32[]{:S(2)}, u32[]{:S(2)}) %collective-permute-start) | collective-permute-done | bytes 131104 | tf_op jit(solution)/shard_map/ppermute | solution.py:313
  9.8 0.6 %copy-done.1 = bf16[2048,256]{1,0:T(8,128)(2,1)S(1)} copy-done((bf16[2048,256]{1,0:T(8,128)(2,1)S(1)}, bf16[2048,256]{1,0:T(8,128)(2,1)}, u32[]{:S(2)}) %copy-start.1) | copy-done | bytes 1048600
  10.4 0.1 copy-done.3
  10.6 0.0 copy-done.5
  10.6 0.0 copy-start.7
  10.6 0.7 %copy-done.7 = f32[2048]{0:T(1024)S(1)} copy-done((f32[2048]{0:T(1024)S(1)}, f32[2048]{0:T(1024)}, u32[]{:S(2)}) %copy-start.7) | copy-done | bytes 8216
  11.3 7.7 %tri_part.2 = (bf16[128,2048]{1,0:T(8,128)(2,1)}, bf16[64,256]{1,0:T(8,128)(2,1)S(1)}) custom-call(s32[1]{0:T(128)} %bitcast.refs_0_.me_ref, f32[8,128]{1,0:T(8,128)S(1)} %stage.1.refs_1_.staged_ref, bf16[128,2048]{1,0:T(8,128)(2,1)S(1)} %copy-done.3, bf16[128,512]{1,0:T(8,128)(2,1)S(1)} %collective-permute-done.refs_3_.prev_ref, ...), custom_call_target="tpu_custom_call" | custom-call | flops 2147483648 | bytes 2097152 | tf_op jit(solution)/shard_map/tri_part/pallas_call | solution.py:152
  19.0 1.9 %collective-permute-start.1 = (bf16[16,256]{1,0:T(8,128)(2,1)S(1)}, bf16[16,256]{1,0:T(8,128)(2,1)S(1)}, u32[]{:S(2)}, u32[]{:S(2)}) collective-permute-start(bf16[16,256]{1,0:T(8,128)(2,1)S(1)} %slice.3), channel_id=1, source_target_pairs={{0,1},{1,2},{2,3},{3,4},{4,5},{5,6},{6,7},{7,8},{8,9},{9,10},{10,1... | collective-permute-start | bytes 24584 | tf_op jit(solution)/shard_map/ppermute | solution.py:313
  20.9 7.7 %tri_part.3 = (bf16[128,2048]{1,0:T(8,128)(2,1)}, bf16[64,256]{1,0:T(8,128)(2,1)S(1)}) custom-call(s32[1]{0:T(128)} %bitcast.refs_0_.me_ref, f32[8,128]{1,0:T(8,128)S(1)} %stage.1.refs_1_.staged_ref, bf16[128,2048]{1,0:T(8,128)(2,1)S(1)} %copy-done.3, bf16[128,512]{1,0:T(8,128)(2,1)S(1)} %collective-permute-done.refs_3_.prev_ref, ...), custom_call_target="tpu_custom_call", output_to_operand_aliasing={{0}: (7, {})} | custom-call | flops 2147483648 | bytes 2097152 | tf_op jit(solution)/shard_map/tri_part/pallas_call | solution.py:152
  28.7 0.0 collective-permute-done.1
  28.7 0.1 fusion.2
  28.8 23.9 %all-gather = bf16[16,127,256]{2,1,0:T(8,128)(2,1)S(1)} all-gather(bf16[1,127,256]{2,1,0:T(8,128)(2,1)S(1)} %fusion.2), channel_id=1, replica_groups=mesh['dp'=32,'seq'=16] {'seq'}, dimensions={0}, use_global_device_ids=true | all-gather | bytes 1105408 | tf_op jit(solution)/shard_map/all_gather | solution.py:330
  52.7 0.0 copy-start.6
  52.7 0.3 reshape.13.far_ref
  53.0 0.7 %copy-done.6 = bf16[128,2048]{1,0:T(8,128)(2,1)S(1)} copy-done((bf16[128,2048]{1,0:T(8,128)(2,1)S(1)}, bf16[128,2048]{1,0:T(8,128)(2,1)}, u32[]{:S(2)}) %copy-start.6) | copy-done | bytes 524312
  53.7 4.3 %causal.1 = bf16[128,2048]{1,0:T(8,128)(2,1)} custom-call(s32[1]{0:T(128)} %bitcast.refs_0_.me_ref, bf16[128,2048]{1,0:T(8,128)(2,1)S(1)} %copy-done.6, bf16[2032,256]{1,0:T(8,128)(2,1)S(1)} %reshape.13.far_ref, bf16[128,256]{1,0:T(8,128)(2,1)S(1)} %pad_maximum_fusion.own_ref), custom_call_target="tpu_custom_call" | custom-call | flops 2147483648 | bytes 3145728 | tf_op jit(solution)/shard_map/causal/pallas_call | solution.py:288
  (3 shorter events, 0.0 us)
Async XLA Ops:
  0.6 9.2 %collective-permute-start = (bf16[128,512]{1,0:T(8,128)(2,1)}, bf16[128,512]{1,0:T(8,128)(2,1)S(1)}, u32[]{:S(2)}, u32[]{:S(2)}) collective-permute-start(bf16[128,512]{1,0:T(8,128)(2,1)} %cur_ref.1), channel_id=1, source_target_pairs={{0,1},{1,2},{2,3},{3,4},{4,5},{5,6},{6,7},{7,8},{8,9},{9,10},{10,1... | collective-permute-start | bytes 393224 | tf_op jit(solution)/shard_map/ppermute | solution.py:313
  6.0 1.2 %copy-start = (bf16[2048,256]{1,0:T(8,128)(2,1)S(1)}, bf16[2048,256]{1,0:T(8,128)(2,1)}, u32[]{:S(2)}) copy-start(bf16[2048,256]{1,0:T(8,128)(2,1)} %weight_ref.1) | copy-start | bytes 3145732
  7.3 1.0 %copy-start.2 = (bf16[128,2048]{1,0:T(8,128)(2,1)S(1)}, bf16[128,2048]{1,0:T(8,128)(2,1)}, u32[]{:S(2)}) copy-start(bf16[128,2048]{1,0:T(8,128)(2,1)} %q_ref.2) | copy-start | bytes 1572868
  8.3 0.9 %copy-start.4 = (bf16[128,512]{1,0:T(8,128)(2,1)S(1)}, bf16[128,512]{1,0:T(8,128)(2,1)}, u32[]{:S(2)}) copy-start(bf16[128,512]{1,0:T(8,128)(2,1)} %cur_ref.1) | copy-start | bytes 393220
  9.2 1.2 %copy-start.1 = (bf16[2048,256]{1,0:T(8,128)(2,1)S(1)}, bf16[2048,256]{1,0:T(8,128)(2,1)}, u32[]{:S(2)}) copy-start(bf16[2048,256]{1,0:T(8,128)(2,1)} %weight_ref.1) | copy-start | bytes 3145732
  9.2 1.4 %copy-start.3 = (bf16[128,2048]{1,0:T(8,128)(2,1)S(1)}, bf16[128,2048]{1,0:T(8,128)(2,1)}, u32[]{:S(2)}) copy-start(bf16[128,2048]{1,0:T(8,128)(2,1)} %q_ref.2) | copy-start | bytes 1572868
  9.2 1.4 %copy-start.5 = (bf16[128,512]{1,0:T(8,128)(2,1)S(1)}, bf16[128,512]{1,0:T(8,128)(2,1)}, u32[]{:S(2)}) copy-start(bf16[128,512]{1,0:T(8,128)(2,1)} %cur_ref.1) | copy-start | bytes 393220
  10.6 0.7 %copy-start.7 = (f32[2048]{0:T(1024)S(1)}, f32[2048]{0:T(1024)}, u32[]{:S(2)}) copy-start(f32[2048]{0:T(1024)} %param.8) | copy-start | bytes 24580
  19.0 9.7 %collective-permute-start.1 = (bf16[16,256]{1,0:T(8,128)(2,1)S(1)}, bf16[16,256]{1,0:T(8,128)(2,1)S(1)}, u32[]{:S(2)}, u32[]{:S(2)}) collective-permute-start(bf16[16,256]{1,0:T(8,128)(2,1)S(1)} %slice.3), channel_id=1, source_target_pairs={{0,1},{1,2},{2,3},{3,4},{4,5},{5,6},{6,7},{7,8},{8,9},{9,10},{10,1... | collective-permute-start | bytes 24584 | tf_op jit(solution)/shard_map/ppermute | solution.py:313
  52.7 1.0 %copy-start.6 = (bf16[128,2048]{1,0:T(8,128)(2,1)S(1)}, bf16[128,2048]{1,0:T(8,128)(2,1)}, u32[]{:S(2)}) copy-start(bf16[128,2048]{1,0:T(8,128)(2,1)} %q_ref.3) | copy-start | bytes 1572868

commit v4 on v3

--- a/solution.py
+++ b/solution.py
@@ -14,117 +14,164 @@
 NEG = -1e30
 SCALE = DIM**-0.5
 EXP2_SCALE = SCALE * 1.4426950408889634
-PIECE = 16
-BLOCK = 16
 NT = (((1,), (1,)), ((), ()))
 
 
 def tri_kernel(
     me_ref, staged_ref, q_ref, prev_ref, cur_ref, gain_ref, weight_ref, held_ref, out_ref, kv_ref,
-    k2_scr, v2_scr, mask_scr, s_scr, top_scr, square_scr, shift_scr, *, first_row, rows,
+    wide_scr, q_scr, k2_scr, v2_scr, rest_scr, s_scr, *, first_row, rows,
 ):
+    half = rows // 2
     first_shard = me_ref[0] == 0
-
-    shift_scr[0:16, :] = prev_ref[W1 - 16 : W1, 2 * DIM :].astype(jnp.float32)
-    shift_scr[16:, :] = cur_ref[:, 2 * DIM :].astype(jnp.float32)
-    for lag in range(W2):
-        at = 16 + first_row - lag
-        k2_scr[lag] = shift_scr[at : at + rows, :DIM].astype(jnp.bfloat16)
-        v2_scr[lag] = shift_scr[at : at + rows, DIM:]
-    row = first_row + lax.broadcasted_iota(jnp.int32, (rows, DIM), 0)
-    col = lax.broadcasted_iota(jnp.int32, (rows, DIM), 1)
-    own = col <= row
-    mask_scr[0] = jnp.where(own, 1.0, 0.0).astype(jnp.bfloat16)
-    k1 = jnp.concatenate([cur_ref[:, :DIM], prev_ref[:, :DIM]], 0)
-    v1 = jnp.concatenate([cur_ref[:, DIM : 2 * DIM], prev_ref[:, DIM : 2 * DIM]], 0)
-
-    blocks = [slice(at, at + BLOCK) for at in range(0, rows, BLOCK)]
-    pieces = [slice(at, at + PIECE) for at in range(0, W2, PIECE)]
-
-    def lanes_of(head):
-        return pl.ds(pl.multiple_of(head * DIM, DIM), DIM)
-
-    def score_step(query, block, lags, slot, top, first):
-        mq = jnp.concatenate([query * k2_scr[lag, block] for lag in range(lags.start, lags.stop)], 0)
-        both = lax.dot_general(mq, k1, NT, preferred_element_type=jnp.float32)
-        row = first_row + block.start + lax.broadcasted_iota(jnp.int32, (BLOCK, DIM), 0)
-        own = lax.broadcasted_iota(jnp.int32, (BLOCK, DIM), 1) <= row
-        for n, lag in enumerate(range(lags.start, lags.stop)):
-            here = both[n * BLOCK : (n + 1) * BLOCK]
-            if first:
-                allowed = own
-                if first_row + block.start < lag:
-                    allowed = own & (lag <= row)
-                score = jnp.where(allowed, here[:, :DIM], NEG)
-            else:
-                score = jnp.where(own, here[:, :DIM], here[:, DIM:])
-            s_scr[slot, lag, block] = score
-            top = score if top is None else jnp.maximum(top, score)
-        return top
-
-    def weigh_step(block, lags, slot, top, total, acc):
-        halves = []
-        mask = mask_scr[0, block]
-        for lag in range(lags.start, lags.stop):
-            weight = jnp.exp2((s_scr[slot, lag, block] - top) * EXP2_SCALE)
-            total = weight if total is None else total + weight
-            rounded = weight.astype(jnp.bfloat16)
-            w_own = rounded * mask
-            halves.append(jnp.concatenate([w_own, rounded - w_own], -1))
-        paired = jnp.dot(jnp.concatenate(halves, 0), v1, preferred_element_type=jnp.float32)
-        for n, lag in enumerate(range(lags.start, lags.stop)):
-            part = paired[n * BLOCK : (n + 1) * BLOCK] * v2_scr[lag, block]
-            acc = part if acc is None else acc + part
-        return total, acc
-
-    def spread(top):
-        return jnp.broadcast_to(jnp.max(top, axis=-1, keepdims=True), top.shape)
-
-    def both_steps(score_head, score_slot, weigh_head, first):
-        for block in blocks:
-            query = q_ref[block, lanes_of(score_head)]
-            next_top = total = acc = None
-            top = top_scr[1 - score_slot, block]
-            for lags in pieces:
-                next_top = score_step(query, block, lags, score_slot, next_top, first)
-                total, acc = weigh_step(block, lags, 1 - score_slot, top, total, acc)
-            top_scr[score_slot, block] = spread(next_top)
-            result = (acc / jnp.sum(total, axis=-1, keepdims=True)).astype(jnp.bfloat16)
-            out_ref[block, lanes_of(weigh_head)] = result
-            wide = result.astype(jnp.float32)
-            square_scr[block] += wide * wide
-
-    def all_heads(first):
-        square_scr[...] = jnp.zeros((rows, DIM), jnp.float32)
-        for block in blocks:
-            top = None
-            for lags in pieces:
-                top = score_step(q_ref[block, lanes_of(0)], block, lags, 0, top, first)
-            top_scr[0, block] = spread(top)
-
-        def pair(k, carried):
-            both_steps(2 * k + 1, 1, 2 * k, first)
-            both_steps(jnp.minimum(2 * k + 2, HEADS - 1), 0, 2 * k + 1, first)
-            return carried
-
-        lax.fori_loop(0, HEADS // 2, pair, 0)
-        return square_scr[...]
-
-    def finish(square):
-        mean = jnp.sum(square, axis=-1, keepdims=True) * (1.0 / (HEADS * DIM))
-        inverse = lax.rsqrt(mean + 1e-6)
-        normed = (out_ref[...].astype(jnp.float32) * inverse * gain_ref[...]).astype(jnp.bfloat16)
-        kv_ref[...] = jnp.dot(
-            normed, weight_ref[...], preferred_element_type=jnp.float32
-        ).astype(jnp.bfloat16)
+    starts = (first_row, first_row + half)
+    sides = (slice(0, DIM), slice(DIM, 2 * DIM))
+
+    for head in range(HEADS):
+        wide_scr[pl.ds(head, rows, stride=HEADS), :] = q_ref[
+            :, head * DIM : (head + 1) * DIM
+        ].astype(jnp.float32)
+    q_scr[...] = wide_scr[...].astype(jnp.bfloat16).reshape(rows, HEADS, DIM)
+    if first_row == 0:
+        seconds = [prev_ref[W1 - W2 :, 2 * DIM :], cur_ref[:rows, 2 * DIM :]]
+    else:
+        seconds = [cur_ref[first_row - W2 : first_row + rows, 2 * DIM :]]
+    seconds = jnp.concatenate(seconds, 0).astype(jnp.float32)
+    for at in range(0, rows + W2, 8):
+        key_two = seconds[at : at + 8, :DIM]
+        val_two = seconds[at : at + 8, DIM:]
+        k2_scr[at : at + 8] = jnp.broadcast_to(key_two[:, None], (8, HEADS, DIM)).astype(
+            jnp.bfloat16
+        )
+        v2_scr[at : at + 8] = jnp.broadcast_to(val_two[:, None], (8, 8, DIM))
+    tile = 16
+    tiles = W1 // tile
+    for n, start in enumerate(starts):
+        now = start // tile
+        for slot in range(tiles - 1):
+            source = (now + 1 + slot) % tiles
+            held = cur_ref if source < now else prev_ref
+            rest_scr[n, slot] = held[source * tile : (source + 1) * tile, : 2 * DIM]
+
+    def ring_of(n, lanes, group, step):
+        place = pl.multiple_of(starts[n] + group * tile, tile)
+        passed = lax.broadcasted_iota(jnp.int32, (tile, DIM), 0) <= step
+        own = cur_ref[pl.ds(place, tile), lanes].astype(jnp.float32)
+        prev = prev_ref[pl.ds(place, tile), lanes].astype(jnp.float32)
+        mixed = jnp.where(passed, own, prev).astype(jnp.bfloat16)
+        whole = [rest_scr[n, slot, :, lanes] for slot in range(tiles - 1)]
+        return jnp.concatenate(whole + [mixed], 0)
+
+    def diagonal(lanes, group, step):
+        zero = jnp.zeros((DIM, DIM), jnp.bfloat16)
+        return jnp.concatenate(
+            [
+                jnp.concatenate([ring_of(0, lanes, group, step), zero], -1),
+                jnp.concatenate([zero, ring_of(1, lanes, group, step)], -1),
+            ],
+            0,
+        )
+
+    def leave(lanes, group):
+        for n, start in enumerate(starts):
+            place = pl.multiple_of(start + group * tile, tile)
+            rest_scr[n, group, :, lanes] = cur_ref[pl.ds(place, tile), lanes]
+
+    def score_step(group, step, slot, first):
+        local = group * tile + step
+        mq = []
+        for lag in range(W2):
+            mq.append(
+                jnp.concatenate(
+                    [
+                        q_scr[n * half + local] * k2_scr[n * half + local + W2 - lag]
+                        for n in range(2)
+                    ],
+                    -1,
+                )
+            )
+        score = lax.dot_general(
+            jnp.concatenate(mq, 0), diagonal(sides[0], group, step), NT, preferred_element_type=jnp.float32
+        ).reshape(W2, HEADS, 2 * DIM)
+        if first:
+            lag = lax.broadcasted_iota(jnp.int32, (W2, HEADS, DIM), 0)
+            col = lax.broadcasted_iota(jnp.int32, (W2, HEADS, DIM), 2)
+            parts = []
+            for n in range(2):
+                row = starts[n] + local
+                seat = jnp.right_shift(col, 4)
+                past = jnp.where(seat + 1 + starts[n] // tile >= tiles, 0, 1)
+                past = jnp.where(seat < group, 0, past)
+                past = jnp.where(seat == tiles - 1, (col & (tile - 1)) - step, past)
+                allowed = (past <= 0) & (lag <= row)
+                parts.append(jnp.where(allowed, score[:, :, sides[n]], NEG))
+            score = jnp.concatenate(parts, -1)
+        s_scr[slot] = score
+        top = jnp.max(score, axis=0)
+        return tuple(jnp.max(top[:, side], axis=-1, keepdims=True) for side in sides)
+
+    def weigh_step(group, step, slot, tops):
+        local = group * tile + step
+        total = [None, None]
+        weights = []
+        for lag in range(W2):
+            pair = []
+            for n in range(2):
+                weight = jnp.exp2((s_scr[slot, lag, :, sides[n]] - tops[n]) * EXP2_SCALE)
+                total[n] = weight if lag == 0 else total[n] + weight
+                pair.append(weight.astype(jnp.bfloat16))
+            weights.append(jnp.concatenate(pair, -1))
+        paired = jnp.dot(
+            jnp.concatenate(weights, 0),
+            diagonal(sides[1], group, step),
+            preferred_element_type=jnp.float32,
+        ).reshape(W2, 2, 8, 2 * DIM)
+        for n in range(2):
+            acc = None
+            for lag in range(W2):
+                part = paired[lag, :, :, sides[n]] * v2_scr[n * half + local + W2 - lag][None]
+                acc = part if acc is None else acc + part
+            result = acc.reshape(HEADS, DIM) / jnp.sum(total[n], axis=-1, keepdims=True)
+            place = pl.multiple_of((n * half + local) * HEADS, HEADS)
+            wide_scr[pl.ds(place, HEADS), :] = result
+
+    def all_queries(first):
+        groups = half // tile
+
+        def one_group(group, tops):
+            for step in range(tile):
+                after = (group, step + 1)
+                if step == tile - 1:
+                    after = (jnp.minimum(group + 1, groups - 1), 0)
+                    leave(sides[0], group)
+                next_tops = score_step(*after, (step + 1) % 2, first)
+                weigh_step(group, step, step % 2, tops)
+                if step == tile - 1:
+                    leave(sides[1], group)
+                tops = next_tops
+            return tops
+
+        lax.fori_loop(0, groups, one_group, score_step(0, 0, 0, first))
 
     @pl.when(first_shard)
     def _():
-        finish(all_heads(True))
+        all_queries(True)
 
     @pl.when(jnp.logical_not(first_shard))
     def _():
-        finish(all_heads(False))
+        all_queries(False)
+
+    square = jnp.zeros((rows, DIM), jnp.float32)
+    for head in range(HEADS):
+        result = wide_scr[pl.ds(head, rows, stride=HEADS), :].astype(jnp.bfloat16)
+        out_ref[:, head * DIM : (head + 1) * DIM] = result
+        wide = result.astype(jnp.float32)
+        square += wide * wide
+    mean = jnp.sum(square, axis=-1, keepdims=True) * (1.0 / (HEADS * DIM))
+    inverse = lax.rsqrt(mean + 1e-6)
+    normed = (out_ref[...].astype(jnp.float32) * inverse * gain_ref[...]).astype(jnp.bfloat16)
+    kv_ref[...] = jnp.dot(
+        normed, weight_ref[...], preferred_element_type=jnp.float32
+    ).astype(jnp.bfloat16)
 
 
 def tri_call(me, staged, tri_query, behind, tri_keys, gain, kv_weight, held, number, rows):
@@ -162,13 +209,12 @@
             jax.ShapeDtypeStruct((rows, 2 * DIM), jnp.bfloat16),
         ],
         scratch_shapes=[
-            pltpu.VMEM((W2, rows, DIM), jnp.bfloat16),
-            pltpu.VMEM((W2, rows, DIM), jnp.float32),
-            pltpu.VMEM((1, rows, DIM), jnp.bfloat16),
-            pltpu.VMEM((2, W2, rows, DIM), jnp.float32),
-            pltpu.VMEM((2, rows, DIM), jnp.float32),
-            pltpu.VMEM((rows, DIM), jnp.float32),
-            pltpu.VMEM((W1 + 16, 2 * DIM), jnp.float32),
+            pltpu.VMEM((rows * HEADS, DIM), jnp.float32),
+            pltpu.VMEM((rows, HEADS, DIM), jnp.bfloat16),
+            pltpu.VMEM((rows + W2, HEADS, DIM), jnp.bfloat16),
+            pltpu.VMEM((rows + W2, 8, DIM), jnp.float32),
+            pltpu.VMEM((2, W1 // 16 - 1, 16, 2 * DIM), jnp.bfloat16),
+            pltpu.VMEM((2, W2, HEADS, 2 * DIM), jnp.float32),
         ],
         input_output_aliases=aliases,
         compiler_params=pltpu.CompilerParams(vmem_limit_bytes=40 * 1024 * 1024),

time: 58.4 us -> 53.3 us (0.913)
  Pallas kernels: 19.7 us -> 14.6 us
    pallas_call x2, Pallas kernels: 15.4 us -> 10.2 us  [tri_call(): pl.pallas_call(kernel, grid=(1,), in_specs=in_specs, out_specs=[pl.BlockS...]
  transfers between devices with their start and end apart: 2 -> 2, of which waited for: 1 -> 1; matrix products, arithmetic and copies ran while one was open for 0% -> 0% of each run, Pallas kernels for 13% -> 10%
where the time goes in v4:
time: 53.3 us; the launch traced here: 52.9 us
  blocking collectives  23.9 us (45%)
  Pallas kernels  14.6 us (27%)
  starting transfers between devices  7.33 us (14%)
  local copies, waits for them, and re-layouts  5.65 us (11%)
  between operations  0.69 us (1%)
  waiting for transfers between devices  0.62 us (1%)
    all_gather x1, blocking collectives, per_device(): far = lax.all_gather(share, 'seq', axis=0, tiled=True)  23.9 us
    pallas_call x2, Pallas kernels, tri_call(): pl.pallas_call(kernel, grid=(1,), in_specs=in_specs, out_specs=[pl.BlockS...  10.2 us
    ppermute x2, starting transfers between devices, passed_along(): return lax.ppermute(block, axis, [(i, i + 1) for i in range(count - 1)])  7.33 us
    unnamed x17, local copies, waits for them, and re-layouts  5.65 us
    pallas_call x1, Pallas kernels, att_call(): pl.pallas_call(functools.partial(att_kernel, rows=rows), grid=(1,), in_sp...  4.44 us
  transfers between devices with their start and end apart: 2, of which 1 were waited for; matrix products, arithmetic and copies ran while one was open for 0% of the time, Pallas kernels for 10%

profile of v4, /device:TPU:1, one launch (start us, length us, event | category | flops | bytes accessed | tf_op | source)
XLA Modules:
  0.0 52.9 jit_solution(6091525481996875433)
XLA Ops:
  0.6 5.4 %collective-permute-start = (bf16[128,512]{1,0:T(8,128)(2,1)}, bf16[128,512]{1,0:T(8,128)(2,1)S(1)}, u32[]{:S(2)}, u32[]{:S(2)}) collective-permute-start(bf16[128,512]{1,0:T(8,128)(2,1)} %cur_ref.1), channel_id=1, source_target_pairs={{0,1},{1,2},{2,3},{3,4},{4,5},{5,6},{6,7},{7,8},{8,9},{9,10},{10,1... | collective-permute-start | bytes 393224 | tf_op jit(solution)/shard_map/ppermute | solution.py:359
  6.0 0.0 copy-start
  6.0 1.2 %copy-done = bf16[2048,256]{1,0:T(8,128)(2,1)S(1)} copy-done((bf16[2048,256]{1,0:T(8,128)(2,1)S(1)}, bf16[2048,256]{1,0:T(8,128)(2,1)}, u32[]{:S(2)}) %copy-start) | copy-done | bytes 1048600
  7.3 0.0 copy-start.2
  7.3 1.0 %copy-done.2 = bf16[128,2048]{1,0:T(8,128)(2,1)S(1)} copy-done((bf16[128,2048]{1,0:T(8,128)(2,1)S(1)}, bf16[128,2048]{1,0:T(8,128)(2,1)}, u32[]{:S(2)}) %copy-start.2) | copy-done | bytes 524312
  8.3 0.0 copy-start.4
  8.3 0.9 %copy-done.4 = bf16[128,512]{1,0:T(8,128)(2,1)S(1)} copy-done((bf16[128,512]{1,0:T(8,128)(2,1)S(1)}, bf16[128,512]{1,0:T(8,128)(2,1)}, u32[]{:S(2)}) %copy-start.4) | copy-done | bytes 131096
  9.2 0.0 copy-start.1
  9.2 0.0 copy-start.3
  9.2 0.0 copy-start.5
  9.2 0.6 %collective-permute-done.refs_3_.prev_ref = bf16[128,512]{1,0:T(8,128)(2,1)S(1)} collective-permute-done((bf16[128,512]{1,0:T(8,128)(2,1)}, bf16[128,512]{1,0:T(8,128)(2,1)S(1)}, u32[]{:S(2)}, u32[]{:S(2)}) %collective-permute-start) | collective-permute-done | bytes 131104 | tf_op jit(solution)/shard_map/ppermute | solution.py:359
  9.8 0.6 %copy-done.1 = bf16[2048,256]{1,0:T(8,128)(2,1)S(1)} copy-done((bf16[2048,256]{1,0:T(8,128)(2,1)S(1)}, bf16[2048,256]{1,0:T(8,128)(2,1)}, u32[]{:S(2)}) %copy-start.1) | copy-done | bytes 1048600
  10.4 0.1 copy-done.3
  10.6 0.0 copy-done.5
  10.6 0.0 copy-start.7
  10.6 0.7 %copy-done.7 = f32[2048]{0:T(1024)S(1)} copy-done((f32[2048]{0:T(1024)S(1)}, f32[2048]{0:T(1024)}, u32[]{:S(2)}) %copy-start.7) | copy-done | bytes 8216
  11.3 5.0 %tri_part.2 = (bf16[128,2048]{1,0:T(8,128)(2,1)}, bf16[64,256]{1,0:T(8,128)(2,1)S(1)}) custom-call(s32[1]{0:T(128)} %bitcast.refs_0_.me_ref, f32[8,128]{1,0:T(8,128)S(1)} %stage.1.refs_1_.staged_ref, bf16[128,2048]{1,0:T(8,128)(2,1)S(1)} %copy-done.3, bf16[128,512]{1,0:T(8,128)(2,1)S(1)} %collective-permute-done.refs_3_.prev_ref, ...), custom_call_target="tpu_custom_call" | custom-call | flops 2147483648 | bytes 2097152 | tf_op jit(solution)/shard_map/tri_part/pallas_call | solution.py:199
  16.3 1.9 %collective-permute-start.1 = (bf16[16,256]{1,0:T(8,128)(2,1)S(1)}, bf16[16,256]{1,0:T(8,128)(2,1)S(1)}, u32[]{:S(2)}, u32[]{:S(2)}) collective-permute-start(bf16[16,256]{1,0:T(8,128)(2,1)S(1)} %slice.3), channel_id=1, source_target_pairs={{0,1},{1,2},{2,3},{3,4},{4,5},{5,6},{6,7},{7,8},{8,9},{9,10},{10,1... | collective-permute-start | bytes 24584 | tf_op jit(solution)/shard_map/ppermute | solution.py:359
  18.2 5.2 %tri_part.3 = (bf16[128,2048]{1,0:T(8,128)(2,1)}, bf16[64,256]{1,0:T(8,128)(2,1)S(1)}) custom-call(s32[1]{0:T(128)} %bitcast.refs_0_.me_ref, f32[8,128]{1,0:T(8,128)S(1)} %stage.1.refs_1_.staged_ref, bf16[128,2048]{1,0:T(8,128)(2,1)S(1)} %copy-done.3, bf16[128,512]{1,0:T(8,128)(2,1)S(1)} %collective-permute-done.refs_3_.prev_ref, ...), custom_call_target="tpu_custom_call", output_to_operand_aliasing={{0}: (7, {})} | custom-call | flops 2147483648 | bytes 2097152 | tf_op jit(solution)/shard_map/tri_part/pallas_call | solution.py:199
  23.4 0.0 collective-permute-done.1
  23.4 0.1 fusion.2
  23.5 23.9 %all-gather = bf16[16,127,256]{2,1,0:T(8,128)(2,1)S(1)} all-gather(bf16[1,127,256]{2,1,0:T(8,128)(2,1)S(1)} %fusion.2), channel_id=1, replica_groups=mesh['dp'=32,'seq'=16] {'seq'}, dimensions={0}, use_global_device_ids=true | all-gather | bytes 1105408 | tf_op jit(solution)/shard_map/all_gather | solution.py:376
  47.4 0.0 copy-start.6
  47.4 0.3 reshape.13.far_ref
  47.7 0.7 %copy-done.6 = bf16[128,2048]{1,0:T(8,128)(2,1)S(1)} copy-done((bf16[128,2048]{1,0:T(8,128)(2,1)S(1)}, bf16[128,2048]{1,0:T(8,128)(2,1)}, u32[]{:S(2)}) %copy-start.6) | copy-done | bytes 524312
  48.5 4.4 %causal.1 = bf16[128,2048]{1,0:T(8,128)(2,1)} custom-call(s32[1]{0:T(128)} %bitcast.refs_0_.me_ref, bf16[128,2048]{1,0:T(8,128)(2,1)S(1)} %copy-done.6, bf16[2032,256]{1,0:T(8,128)(2,1)S(1)} %reshape.13.far_ref, bf16[128,256]{1,0:T(8,128)(2,1)S(1)} %pad_maximum_fusion.own_ref), custom_call_target="tpu_custom_call" | custom-call | flops 2147483648 | bytes 3145728 | tf_op jit(solution)/shard_map/causal/pallas_call | solution.py:334
  (3 shorter events, 0.0 us)
Async XLA Ops:
  0.6 9.2 %collective-permute-start = (bf16[128,512]{1,0:T(8,128)(2,1)}, bf16[128,512]{1,0:T(8,128)(2,1)S(1)}, u32[]{:S(2)}, u32[]{:S(2)}) collective-permute-start(bf16[128,512]{1,0:T(8,128)(2,1)} %cur_ref.1), channel_id=1, source_target_pairs={{0,1},{1,2},{2,3},{3,4},{4,5},{5,6},{6,7},{7,8},{8,9},{9,10},{10,1... | collective-permute-start | bytes 393224 | tf_op jit(solution)/shard_map/ppermute | solution.py:359
  6.0 1.2 %copy-start = (bf16[2048,256]{1,0:T(8,128)(2,1)S(1)}, bf16[2048,256]{1,0:T(8,128)(2,1)}, u32[]{:S(2)}) copy-start(bf16[2048,256]{1,0:T(8,128)(2,1)} %weight_ref.1) | copy-start | bytes 3145732
  7.3 1.0 %copy-start.2 = (bf16[128,2048]{1,0:T(8,128)(2,1)S(1)}, bf16[128,2048]{1,0:T(8,128)(2,1)}, u32[]{:S(2)}) copy-start(bf16[128,2048]{1,0:T(8,128)(2,1)} %q_ref.2) | copy-start | bytes 1572868
  8.3 0.9 %copy-start.4 = (bf16[128,512]{1,0:T(8,128)(2,1)S(1)}, bf16[128,512]{1,0:T(8,128)(2,1)}, u32[]{:S(2)}) copy-start(bf16[128,512]{1,0:T(8,128)(2,1)} %cur_ref.1) | copy-start | bytes 393220
  9.2 1.2 %copy-start.1 = (bf16[2048,256]{1,0:T(8,128)(2,1)S(1)}, bf16[2048,256]{1,0:T(8,128)(2,1)}, u32[]{:S(2)}) copy-start(bf16[2048,256]{1,0:T(8,128)(2,1)} %weight_ref.1) | copy-start | bytes 3145732
  9.2 1.4 %copy-start.3 = (bf16[128,2048]{1,0:T(8,128)(2,1)S(1)}, bf16[128,2048]{1,0:T(8,128)(2,1)}, u32[]{:S(2)}) copy-start(bf16[128,2048]{1,0:T(8,128)(2,1)} %q_ref.2) | copy-start | bytes 1572868
  9.2 1.4 %copy-start.5 = (bf16[128,512]{1,0:T(8,128)(2,1)S(1)}, bf16[128,512]{1,0:T(8,128)(2,1)}, u32[]{:S(2)}) copy-start(bf16[128,512]{1,0:T(8,128)(2,1)} %cur_ref.1) | copy-start | bytes 393220
  10.6 0.7 %copy-start.7 = (f32[2048]{0:T(1024)S(1)}, f32[2048]{0:T(1024)}, u32[]{:S(2)}) copy-start(f32[2048]{0:T(1024)} %param.8) | copy-start | bytes 24580
  16.3 7.1 %collective-permute-start.1 = (bf16[16,256]{1,0:T(8,128)(2,1)S(1)}, bf16[16,256]{1,0:T(8,128)(2,1)S(1)}, u32[]{:S(2)}, u32[]{:S(2)}) collective-permute-start(bf16[16,256]{1,0:T(8,128)(2,1)S(1)} %slice.3), channel_id=1, source_target_pairs={{0,1},{1,2},{2,3},{3,4},{4,5},{5,6},{6,7},{7,8},{8,9},{9,10},{10,1... | collective-permute-start | bytes 24584 | tf_op jit(solution)/shard_map/ppermute | solution.py:359
  47.4 1.0 %copy-start.6 = (bf16[128,2048]{1,0:T(8,128)(2,1)S(1)}, bf16[128,2048]{1,0:T(8,128)(2,1)}, u32[]{:S(2)}) copy-start(bf16[128,2048]{1,0:T(8,128)(2,1)} %q_ref.3) | copy-start | bytes 1572868

commit v5 on v4

--- a/solution.py
+++ b/solution.py
@@ -265,60 +265,71 @@
                 return own_ref[:, lanes]
             return far_ref[tile * DIM : (tile + 1) * DIM, lanes]
 
-        def score_step(query, slot, tile, top):
+        heads = max(1, min(4, shards // tiles))
+
+        def gather_queries(item):
+            return jnp.concatenate([q_ref[:, lanes_of(item * heads + h)] for h in range(heads)], 0)
+
+        def score_step(query, slot, tile, tops):
             keys = [of_tile(tile, slice(0, DIM)), of_tile(tile + 1, slice(0, DIM))]
             both = lax.dot_general(
                 query, jnp.concatenate(keys, 0), NT, preferred_element_type=jnp.float32
             )
+            for h in range(heads):
+                for n in range(2):
+                    score = both[h * rows : (h + 1) * rows, n * DIM : (n + 1) * DIM]
+                    if tile + n == before:
+                        row = lax.broadcasted_iota(jnp.int32, (rows, DIM), 0)
+                        col = lax.broadcasted_iota(jnp.int32, (rows, DIM), 1)
+                        score = jnp.where(col <= row, score, NEG)
+                    else:
+                        score = jnp.minimum(score, caps[tile + n])
+                    s_scr[slot, h * tiles + tile + n] = score
+                    tops[h] = score if tops[h] is None else jnp.maximum(tops[h], score)
+
+        def weigh_step(slot, tile, h, top, total, weights):
             for n in range(2):
-                score = both[:, n * DIM : (n + 1) * DIM]
-                if tile + n == before:
-                    row = lax.broadcasted_iota(jnp.int32, (rows, DIM), 0)
-                    col = lax.broadcasted_iota(jnp.int32, (rows, DIM), 1)
-                    score = jnp.where(col <= row, score, NEG)
-                else:
-                    score = jnp.minimum(score, caps[tile + n])
-                s_scr[slot, tile + n] = score
-                top = score if top is None else jnp.maximum(top, score)
-            return top
-
-        def weigh_step(slot, tile, top, total, weights):
-            for n in range(2):
-                weight = jnp.exp2((s_scr[slot, tile + n] - top) * EXP2_SCALE)
+                weight = jnp.exp2((s_scr[slot, h * tiles + tile + n] - top) * EXP2_SCALE)
                 total = weight if total is None else total + weight
-                weights.append(weight.astype(jnp.bfloat16))
+                weights[h].append(weight.astype(jnp.bfloat16))
             return total
 
-        def settle(slot, top):
-            top_scr[slot] = jnp.broadcast_to(jnp.max(top, axis=-1, keepdims=True), (rows, DIM))
-
-        def both_steps(score_head, score_slot, weigh_head):
-            query = q_ref[:, lanes_of(score_head)]
-            next_top = total = None
-            weights = []
-            top = top_scr[1 - score_slot]
+        def settle(slot, tops):
+            for h in range(heads):
+                top = jnp.max(tops[h], axis=-1, keepdims=True)
+                top_scr[slot, h] = jnp.broadcast_to(top, (rows, DIM))
+
+        def both_steps(score_item, score_slot, weigh_item):
+            query = gather_queries(score_item)
+            next_tops, totals = [None] * heads, [None] * heads
+            weights = [[] for _ in range(heads)]
             for tile in range(0, tiles, 2):
-                next_top = score_step(query, score_slot, tile, next_top)
-                total = weigh_step(1 - score_slot, tile, top, total, weights)
-            settle(score_slot, next_top)
+                score_step(query, score_slot, tile, next_tops)
+                for h in range(heads):
+                    top = top_scr[1 - score_slot, h]
+                    totals[h] = weigh_step(1 - score_slot, tile, h, top, totals[h], weights)
+            settle(score_slot, next_tops)
             values = jnp.concatenate([of_tile(t, slice(DIM, 2 * DIM)) for t in range(tiles)], 0)
-            acc = jnp.dot(
-                jnp.concatenate(weights, -1), values, preferred_element_type=jnp.float32
-            )
-            result = acc / jnp.sum(total, axis=-1, keepdims=True)
-            out_ref[:, lanes_of(weigh_head)] = result.astype(jnp.bfloat16)
-
-        top = None
+            stacked = jnp.concatenate([jnp.concatenate(w, -1) for w in weights], 0)
+            acc = jnp.dot(stacked, values, preferred_element_type=jnp.float32)
+            for h in range(heads):
+                total = jnp.sum(totals[h], axis=-1, keepdims=True)
+                result = acc[h * rows : (h + 1) * rows] / total
+                out_ref[:, lanes_of(weigh_item * heads + h)] = result.astype(jnp.bfloat16)
+
+        items = HEADS // heads
+        tops = [None] * heads
+        query = gather_queries(0)
         for tile in range(0, tiles, 2):
-            top = score_step(q_ref[:, lanes_of(0)], 0, tile, top)
-        settle(0, top)
+            score_step(query, 0, tile, tops)
+        settle(0, tops)
 
         def pair(k, carried):
             both_steps(2 * k + 1, 1, 2 * k)
-            both_steps(jnp.minimum(2 * k + 2, HEADS - 1), 0, 2 * k + 1)
+            both_steps(jnp.minimum(2 * k + 2, items - 1), 0, 2 * k + 1)
             return carried
 
-        lax.fori_loop(0, HEADS // 2, pair, 0)
+        lax.fori_loop(0, items // 2, pair, 0)
 
     lowest = 0
     for before in range(1, shards + 1, SPAN):
@@ -344,7 +355,7 @@
         out_shape=jax.ShapeDtypeStruct(att_query.shape, jnp.bfloat16),
         scratch_shapes=[
             pltpu.VMEM((2, tokens // DIM, rows, DIM), jnp.float32),
-            pltpu.VMEM((2, rows, DIM), jnp.float32),
+            pltpu.VMEM((2, 4, rows, DIM), jnp.float32),
         ],
         compiler_params=pltpu.CompilerParams(vmem_limit_bytes=48 * 1024 * 1024),
         cost_estimate=pl.CostEstimate(

time: 53.3 us -> 51.2 us (0.961)
  Pallas kernels: 14.6 us -> 12.5 us
    pallas_call x1, Pallas kernels: 4.44 us -> 2.38 us  [att_call(): pl.pallas_call(functools.partial(att_kernel, rows=rows), grid=(1,), in_sp...]
where the time goes in v5:
time: 51.2 us; the launch traced here: 50.9 us
  blocking collectives  23.9 us (47%)
  Pallas kernels  12.5 us (24%)
  starting transfers between devices  7.33 us (14%)
  local copies, waits for them, and re-layouts  5.65 us (11%)
  between operations  0.69 us (1%)
  waiting for transfers between devices  0.62 us (1%)
    all_gather x1, blocking collectives, per_device(): far = lax.all_gather(share, 'seq', axis=0, tiled=True)  23.9 us
    pallas_call x2, Pallas kernels, tri_call(): pl.pallas_call(kernel, grid=(1,), in_specs=in_specs, out_specs=[pl.BlockS...  10.2 us
    ppermute x2, starting transfers between devices, passed_along(): return lax.ppermute(block, axis, [(i, i + 1) for i in range(count - 1)])  7.33 us
    unnamed x17, local copies, waits for them, and re-layouts  5.65 us
    pallas_call x1, Pallas kernels, att_call(): pl.pallas_call(functools.partial(att_kernel, rows=rows), grid=(1,), in_sp...  2.38 us
  transfers between devices with their start and end apart: 2, of which 1 were waited for; matrix products, arithmetic and copies ran while one was open for 0% of the time, Pallas kernels for 10%

profile of v5, /device:TPU:1, one launch (start us, length us, event | category | flops | bytes accessed | tf_op | source)
XLA Modules:
  0.0 50.9 jit_solution(17988150828335613995)
XLA Ops:
  0.6 5.4 %collective-permute-start = (bf16[128,512]{1,0:T(8,128)(2,1)}, bf16[128,512]{1,0:T(8,128)(2,1)S(1)}, u32[]{:S(2)}, u32[]{:S(2)}) collective-permute-start(bf16[128,512]{1,0:T(8,128)(2,1)} %cur_ref.1), channel_id=1, source_target_pairs={{0,1},{1,2},{2,3},{3,4},{4,5},{5,6},{6,7},{7,8},{8,9},{9,10},{10,1... | collective-permute-start | bytes 393224 | tf_op jit(solution)/shard_map/ppermute | solution.py:370
  6.0 0.0 copy-start
  6.0 1.2 %copy-done = bf16[2048,256]{1,0:T(8,128)(2,1)S(1)} copy-done((bf16[2048,256]{1,0:T(8,128)(2,1)S(1)}, bf16[2048,256]{1,0:T(8,128)(2,1)}, u32[]{:S(2)}) %copy-start) | copy-done | bytes 1048600
  7.3 0.0 copy-start.2
  7.3 1.0 %copy-done.2 = bf16[128,2048]{1,0:T(8,128)(2,1)S(1)} copy-done((bf16[128,2048]{1,0:T(8,128)(2,1)S(1)}, bf16[128,2048]{1,0:T(8,128)(2,1)}, u32[]{:S(2)}) %copy-start.2) | copy-done | bytes 524312
  8.3 0.0 copy-start.4
  8.3 0.9 %copy-done.4 = bf16[128,512]{1,0:T(8,128)(2,1)S(1)} copy-done((bf16[128,512]{1,0:T(8,128)(2,1)S(1)}, bf16[128,512]{1,0:T(8,128)(2,1)}, u32[]{:S(2)}) %copy-start.4) | copy-done | bytes 131096
  9.2 0.0 copy-start.1
  9.2 0.0 copy-start.3
  9.2 0.0 copy-start.5
  9.2 0.6 %collective-permute-done.refs_3_.prev_ref = bf16[128,512]{1,0:T(8,128)(2,1)S(1)} collective-permute-done((bf16[128,512]{1,0:T(8,128)(2,1)}, bf16[128,512]{1,0:T(8,128)(2,1)S(1)}, u32[]{:S(2)}, u32[]{:S(2)}) %collective-permute-start) | collective-permute-done | bytes 131104 | tf_op jit(solution)/shard_map/ppermute | solution.py:370
  9.8 0.6 %copy-done.1 = bf16[2048,256]{1,0:T(8,128)(2,1)S(1)} copy-done((bf16[2048,256]{1,0:T(8,128)(2,1)S(1)}, bf16[2048,256]{1,0:T(8,128)(2,1)}, u32[]{:S(2)}) %copy-start.1) | copy-done | bytes 1048600
  10.4 0.1 copy-done.3
  10.6 0.0 copy-done.5
  10.6 0.0 copy-start.7
  10.6 0.7 %copy-done.7 = f32[2048]{0:T(1024)S(1)} copy-done((f32[2048]{0:T(1024)S(1)}, f32[2048]{0:T(1024)}, u32[]{:S(2)}) %copy-start.7) | copy-done | bytes 8216
  11.3 5.0 %tri_part.2 = (bf16[128,2048]{1,0:T(8,128)(2,1)}, bf16[64,256]{1,0:T(8,128)(2,1)S(1)}) custom-call(s32[1]{0:T(128)} %bitcast.refs_0_.me_ref, f32[8,128]{1,0:T(8,128)S(1)} %stage.1.refs_1_.staged_ref, bf16[128,2048]{1,0:T(8,128)(2,1)S(1)} %copy-done.3, bf16[128,512]{1,0:T(8,128)(2,1)S(1)} %collective-permute-done.refs_3_.prev_ref, ...), custom_call_target="tpu_custom_call" | custom-call | flops 2147483648 | bytes 2097152 | tf_op jit(solution)/shard_map/tri_part/pallas_call | solution.py:199
  16.3 1.9 %collective-permute-start.1 = (bf16[16,256]{1,0:T(8,128)(2,1)S(1)}, bf16[16,256]{1,0:T(8,128)(2,1)S(1)}, u32[]{:S(2)}, u32[]{:S(2)}) collective-permute-start(bf16[16,256]{1,0:T(8,128)(2,1)S(1)} %slice.3), channel_id=1, source_target_pairs={{0,1},{1,2},{2,3},{3,4},{4,5},{5,6},{6,7},{7,8},{8,9},{9,10},{10,1... | collective-permute-start | bytes 24584 | tf_op jit(solution)/shard_map/ppermute | solution.py:370
  18.2 5.2 %tri_part.3 = (bf16[128,2048]{1,0:T(8,128)(2,1)}, bf16[64,256]{1,0:T(8,128)(2,1)S(1)}) custom-call(s32[1]{0:T(128)} %bitcast.refs_0_.me_ref, f32[8,128]{1,0:T(8,128)S(1)} %stage.1.refs_1_.staged_ref, bf16[128,2048]{1,0:T(8,128)(2,1)S(1)} %copy-done.3, bf16[128,512]{1,0:T(8,128)(2,1)S(1)} %collective-permute-done.refs_3_.prev_ref, ...), custom_call_target="tpu_custom_call", output_to_operand_aliasing={{0}: (7, {})} | custom-call | flops 2147483648 | bytes 2097152 | tf_op jit(solution)/shard_map/tri_part/pallas_call | solution.py:199
  23.4 0.0 collective-permute-done.1
  23.4 0.1 fusion.2
  23.5 23.9 %all-gather = bf16[16,127,256]{2,1,0:T(8,128)(2,1)S(1)} all-gather(bf16[1,127,256]{2,1,0:T(8,128)(2,1)S(1)} %fusion.2), channel_id=1, replica_groups=mesh['dp'=32,'seq'=16] {'seq'}, dimensions={0}, use_global_device_ids=true | all-gather | bytes 1105408 | tf_op jit(solution)/shard_map/all_gather | solution.py:387
  47.4 0.0 copy-start.6
  47.4 0.3 reshape.13.far_ref
  47.7 0.7 %copy-done.6 = bf16[128,2048]{1,0:T(8,128)(2,1)S(1)} copy-done((bf16[128,2048]{1,0:T(8,128)(2,1)S(1)}, bf16[128,2048]{1,0:T(8,128)(2,1)}, u32[]{:S(2)}) %copy-start.6) | copy-done | bytes 524312
  48.5 2.4 %causal.1 = bf16[128,2048]{1,0:T(8,128)(2,1)} custom-call(s32[1]{0:T(128)} %bitcast.refs_0_.me_ref, bf16[128,2048]{1,0:T(8,128)(2,1)S(1)} %copy-done.6, bf16[2032,256]{1,0:T(8,128)(2,1)S(1)} %reshape.13.far_ref, bf16[128,256]{1,0:T(8,128)(2,1)S(1)} %pad_maximum_fusion.own_ref), custom_call_target="tpu_custom_call" | custom-call | flops 2147483648 | bytes 3145728 | tf_op jit(solution)/shard_map/causal/pallas_call | solution.py:345
  (3 shorter events, 0.0 us)
Async XLA Ops:
  0.6 9.2 %collective-permute-start = (bf16[128,512]{1,0:T(8,128)(2,1)}, bf16[128,512]{1,0:T(8,128)(2,1)S(1)}, u32[]{:S(2)}, u32[]{:S(2)}) collective-permute-start(bf16[128,512]{1,0:T(8,128)(2,1)} %cur_ref.1), channel_id=1, source_target_pairs={{0,1},{1,2},{2,3},{3,4},{4,5},{5,6},{6,7},{7,8},{8,9},{9,10},{10,1... | collective-permute-start | bytes 393224 | tf_op jit(solution)/shard_map/ppermute | solution.py:370
  6.0 1.2 %copy-start = (bf16[2048,256]{1,0:T(8,128)(2,1)S(1)}, bf16[2048,256]{1,0:T(8,128)(2,1)}, u32[]{:S(2)}) copy-start(bf16[2048,256]{1,0:T(8,128)(2,1)} %weight_ref.1) | copy-start | bytes 3145732
  7.3 1.0 %copy-start.2 = (bf16[128,2048]{1,0:T(8,128)(2,1)S(1)}, bf16[128,2048]{1,0:T(8,128)(2,1)}, u32[]{:S(2)}) copy-start(bf16[128,2048]{1,0:T(8,128)(2,1)} %q_ref.2) | copy-start | bytes 1572868
  8.3 0.9 %copy-start.4 = (bf16[128,512]{1,0:T(8,128)(2,1)S(1)}, bf16[128,512]{1,0:T(8,128)(2,1)}, u32[]{:S(2)}) copy-start(bf16[128,512]{1,0:T(8,128)(2,1)} %cur_ref.1) | copy-start | bytes 393220
  9.2 1.2 %copy-start.1 = (bf16[2048,256]{1,0:T(8,128)(2,1)S(1)}, bf16[2048,256]{1,0:T(8,128)(2,1)}, u32[]{:S(2)}) copy-start(bf16[2048,256]{1,0:T(8,128)(2,1)} %weight_ref.1) | copy-start | bytes 3145732
  9.2 1.4 %copy-start.3 = (bf16[128,2048]{1,0:T(8,128)(2,1)S(1)}, bf16[128,2048]{1,0:T(8,128)(2,1)}, u32[]{:S(2)}) copy-start(bf16[128,2048]{1,0:T(8,128)(2,1)} %q_ref.2) | copy-start | bytes 1572868
  9.2 1.4 %copy-start.5 = (bf16[128,512]{1,0:T(8,128)(2,1)S(1)}, bf16[128,512]{1,0:T(8,128)(2,1)}, u32[]{:S(2)}) copy-start(bf16[128,512]{1,0:T(8,128)(2,1)} %cur_ref.1) | copy-start | bytes 393220
  10.6 0.7 %copy-start.7 = (f32[2048]{0:T(1024)S(1)}, f32[2048]{0:T(1024)}, u32[]{:S(2)}) copy-start(f32[2048]{0:T(1024)} %param.8) | copy-start | bytes 24580
  16.3 7.1 %collective-permute-start.1 = (bf16[16,256]{1,0:T(8,128)(2,1)S(1)}, bf16[16,256]{1,0:T(8,128)(2,1)S(1)}, u32[]{:S(2)}, u32[]{:S(2)}) collective-permute-start(bf16[16,256]{1,0:T(8,128)(2,1)S(1)} %slice.3), channel_id=1, source_target_pairs={{0,1},{1,2},{2,3},{3,4},{4,5},{5,6},{6,7},{7,8},{8,9},{9,10},{10,1... | collective-permute-start | bytes 24584 | tf_op jit(solution)/shard_map/ppermute | solution.py:370
  47.4 1.0 %copy-start.6 = (bf16[128,2048]{1,0:T(8,128)(2,1)S(1)}, bf16[128,2048]{1,0:T(8,128)(2,1)}, u32[]{:S(2)}) copy-start(bf16[128,2048]{1,0:T(8,128)(2,1)} %q_ref.3) | copy-start | bytes 1572868

commit v6 on v5

--- a/solution.py
+++ b/solution.py
@@ -174,7 +174,7 @@
     ).astype(jnp.bfloat16)
 
 
-def tri_call(me, staged, tri_query, behind, tri_keys, gain, kv_weight, held, number, rows):
+def tri_call(me, staged, tri_query, behind, tri_keys, gain, kv_weight, held, number, rows, relayed=None):
     token_rows, width = tri_query.shape
     whole = lambda shape: pl.BlockSpec(shape, lambda i: (0,) * len(shape))
     in_specs = [
@@ -189,13 +189,24 @@
     args = [me, staged, tri_query, behind, tri_keys, gain, kv_weight]
     body = functools.partial(tri_kernel, first_row=number * rows, rows=rows)
     aliases = {}
+    more_specs, more_shapes, more_scratch = [], [], []
     if held is None:
         kernel = lambda *refs: body(*refs[:7], None, *refs[7:])
     else:
-        kernel = body
+
+        def kernel(*refs):
+            copy = pltpu.make_async_copy(refs[8], refs[11], refs[-1])
+            copy.start()
+            body(*refs[:8], *refs[9:11], *refs[12:-1])
+            copy.wait()
+
         in_specs.append(pl.BlockSpec(memory_space=pl.ANY))
-        args.append(held)
+        in_specs.append(pl.BlockSpec(memory_space=pltpu.HBM))
+        args += [held, relayed]
         aliases = {7: 0}
+        more_specs = [pl.BlockSpec(memory_space=pl.ANY)]
+        more_shapes = [jax.ShapeDtypeStruct(relayed.shape, relayed.dtype)]
+        more_scratch = [pltpu.SemaphoreType.DMA]
     return pl.pallas_call(
         kernel,
         grid=(1,),
@@ -203,10 +214,12 @@
         out_specs=[
             pl.BlockSpec((rows, width), lambda i: (number, 0)),
             whole((rows, 2 * DIM)),
+            *more_specs,
         ],
         out_shape=[
             jax.ShapeDtypeStruct((token_rows, width), jnp.bfloat16),
             jax.ShapeDtypeStruct((rows, 2 * DIM), jnp.bfloat16),
+            *more_shapes,
         ],
         scratch_shapes=[
             pltpu.VMEM((rows * HEADS, DIM), jnp.float32),
@@ -215,6 +228,7 @@
             pltpu.VMEM((rows + W2, 8, DIM), jnp.float32),
             pltpu.VMEM((2, W1 // 16 - 1, 16, 2 * DIM), jnp.bfloat16),
             pltpu.VMEM((2, W2, HEADS, 2 * DIM), jnp.float32),
+            *more_scratch,
         ],
         input_output_aliases=aliases,
         compiler_params=pltpu.CompilerParams(vmem_limit_bytes=40 * 1024 * 1024),
@@ -378,14 +392,16 @@
     place = jnp.reshape(me, (1,)).astype(jnp.int32)
     gain = norm_gain.reshape(1, -1)
     behind = passed_along(tri_keys, "seq")
-    staged = stage_call(tri_query, tri_keys, kv_weight)
+    staged = stage_call(tri_query, tri_keys, gain, kv_weight)
     held, kv_late = tri_call(place, staged, tri_query, behind, tri_keys, gain, kv_weight, None, 1, half)
     before = passed_along(kv_late[half - shards :], "seq")
-    tri_out, kv_early = tri_call(place, staged, tri_query, behind, tri_keys, gain, kv_weight, held, 0, half)
+    tri_out, kv_early, near_query = tri_call(
+        place, staged, tri_query, behind, tri_keys, gain, kv_weight, held, 0, half, att_query
+    )
     own = jnp.concatenate([kv_early, kv_late], 0)
     share = lax.dynamic_slice_in_dim(jnp.concatenate([before, own], 0), shards - me, rows - 1, 0)
     far = lax.all_gather(share, "seq", axis=0, tiled=True)
-    attended = att_call(place, att_query, far, own)
+    attended = att_call(place, near_query, far, own)
     return (tri_out, attended)
 
 

time: 51.2 us -> 50 us (0.977)
  local copies, waits for them, and re-layouts: 5.65 us -> 4.24 us
    unnamed x17, local copies, waits for them, and re-layouts: 5.65 us -> 4.24 us
  transfers between devices with their start and end apart: 2 -> 2, of which waited for: 1 -> 1; matrix products, arithmetic and copies ran while one was open for 0% -> 0% of each run, Pallas kernels for 10% -> 11%
where the time goes in v6:
time: 50 us; the launch traced here: 49.7 us
  blocking collectives  23.9 us (48%)
  Pallas kernels  12.8 us (26%)
  starting transfers between devices  7.33 us (15%)
  local copies, waits for them, and re-layouts  4.24 us (8%)
  between operations  0.73 us (1%)
  waiting for transfers between devices  0.61 us (1%)
    all_gather x1, blocking collectives, per_device(): far = lax.all_gather(share, 'seq', axis=0, tiled=True)  23.9 us
    pallas_call x2, Pallas kernels, tri_call(): pl.pallas_call(kernel, grid=(1,), in_specs=in_specs, out_specs=[pl.BlockS...  10.4 us
    ppermute x2, starting transfers between devices, passed_along(): return lax.ppermute(block, axis, [(i, i + 1) for i in range(count - 1)])  7.33 us
    unnamed x17, local copies, waits for them, and re-layouts  4.24 us
    pallas_call x1, Pallas kernels, att_call(): pl.pallas_call(functools.partial(att_kernel, rows=rows), grid=(1,), in_sp...  2.39 us
  transfers between devices with their start and end apart: 2, of which 1 were waited for; matrix products, arithmetic and copies ran while one was open for 0% of the time, Pallas kernels for 11%

profile of v6, /device:TPU:1, one launch (start us, length us, event | category | flops | bytes accessed | tf_op | source)
XLA Modules:
  0.0 49.7 jit_solution(5541522386551044810)
XLA Ops:
  0.6 0.0 copy-start.6
  0.6 5.4 %collective-permute-start = (bf16[128,512]{1,0:T(8,128)(2,1)}, bf16[128,512]{1,0:T(8,128)(2,1)S(1)}, u32[]{:S(2)}, u32[]{:S(2)}) collective-permute-start(bf16[128,512]{1,0:T(8,128)(2,1)} %refs_4_.3), channel_id=1, source_target_pairs={{0,1},{1,2},{2,3},{3,4},{4,5},{5,6},{6,7},{7,8},{8,9},{9,10},{10,1... | collective-permute-start | bytes 393224 | tf_op jit(solution)/shard_map/ppermute | solution.py:384
  6.0 0.0 copy-done.6
  6.1 0.0 copy-start
  6.1 1.2 %copy-done = bf16[2048,256]{1,0:T(8,128)(2,1)S(1)} copy-done((bf16[2048,256]{1,0:T(8,128)(2,1)S(1)}, bf16[2048,256]{1,0:T(8,128)(2,1)}, u32[]{:S(2)}) %copy-start) | copy-done | bytes 1048600
  7.3 0.0 copy-start.2
  7.3 1.0 %copy-done.2 = bf16[128,2048]{1,0:T(8,128)(2,1)S(1)} copy-done((bf16[128,2048]{1,0:T(8,128)(2,1)S(1)}, bf16[128,2048]{1,0:T(8,128)(2,1)}, u32[]{:S(2)}) %copy-start.2) | copy-done | bytes 524312
  8.3 0.0 copy-start.4
  8.3 0.9 %copy-done.4 = bf16[128,512]{1,0:T(8,128)(2,1)S(1)} copy-done((bf16[128,512]{1,0:T(8,128)(2,1)S(1)}, bf16[128,512]{1,0:T(8,128)(2,1)}, u32[]{:S(2)}) %copy-start.4) | copy-done | bytes 131096
  9.2 0.0 copy-start.1
  9.2 0.0 copy-start.3
  9.2 0.0 copy-start.5
  9.2 0.6 %collective-permute-done.refs_3_ = bf16[128,512]{1,0:T(8,128)(2,1)S(1)} collective-permute-done((bf16[128,512]{1,0:T(8,128)(2,1)}, bf16[128,512]{1,0:T(8,128)(2,1)S(1)}, u32[]{:S(2)}, u32[]{:S(2)}) %collective-permute-start) | collective-permute-done | bytes 131104 | tf_op jit(solution)/shard_map/ppermute | solution.py:384
  9.8 0.6 %copy-done.1 = bf16[2048,256]{1,0:T(8,128)(2,1)S(1)} copy-done((bf16[2048,256]{1,0:T(8,128)(2,1)S(1)}, bf16[2048,256]{1,0:T(8,128)(2,1)}, u32[]{:S(2)}) %copy-start.1) | copy-done | bytes 1048600
  10.5 0.1 copy-done.3
  10.6 0.0 copy-done.5
  10.6 0.0 copy-start.7
  10.6 5.0 %tri_part.2 = (bf16[128,2048]{1,0:T(8,128)(2,1)}, bf16[64,256]{1,0:T(8,128)(2,1)S(1)}) custom-call(s32[1]{0:T(128)} %bitcast.refs_0_.me_ref, f32[8,128]{1,0:T(8,128)S(1)} %stage.1.refs_1_, bf16[128,2048]{1,0:T(8,128)(2,1)S(1)} %copy-done.3, bf16[128,512]{1,0:T(8,128)(2,1)S(1)} %collective-permute-done.refs_3_, bf16[128,512]{1,0:T(8,128)(2,1)S(1)} %copy-done.5, ...), custom_call_target="tpu_custom_call" | custom-call | flops 2147483648 | bytes 2097152 | tf_op jit(solution)/shard_map/tri_part/pallas_call | solution.py:210
  15.6 1.9 %collective-permute-start.1 = (bf16[16,256]{1,0:T(8,128)(2,1)S(1)}, bf16[16,256]{1,0:T(8,128)(2,1)S(1)}, u32[]{:S(2)}, u32[]{:S(2)}) collective-permute-start(bf16[16,256]{1,0:T(8,128)(2,1)S(1)} %slice.3), channel_id=1, source_target_pairs={{0,1},{1,2},{2,3},{3,4},{4,5},{5,6},{6,7},{7,8},{8,9},{9,10},{10,1... | collective-permute-start | bytes 24584 | tf_op jit(solution)/shard_map/ppermute | solution.py:384
  17.6 0.0 copy-done.7
  17.6 5.4 %tri_part.3 = (bf16[128,2048]{1,0:T(8,128)(2,1)}, bf16[64,256]{1,0:T(8,128)(2,1)S(1)}, bf16[128,2048]{1,0:T(8,128)(2,1)S(1)}) custom-call(s32[1]{0:T(128)} %bitcast.refs_0_.me_ref, f32[8,128]{1,0:T(8,128)S(1)} %stage.1.refs_1_, bf16[128,2048]{1,0:T(8,128)(2,1)S(1)} %copy-done.3, ...), custom_call_target="tpu_custom_call", output_to_operand_aliasing={{0}: (7, {})} | custom-call | flops 2147483648 | bytes 2097152 | tf_op jit(solution)/shard_map/tri_part/pallas_call | solution.py:210
  23.0 0.0 collective-permute-done.1
  23.0 0.1 fusion.2
  23.1 23.9 %all-gather = bf16[16,127,256]{2,1,0:T(8,128)(2,1)S(1)} all-gather(bf16[1,127,256]{2,1,0:T(8,128)(2,1)S(1)} %fusion.2), channel_id=1, replica_groups=mesh['dp'=32,'seq'=16] {'seq'}, dimensions={0}, use_global_device_ids=true | all-gather | bytes 1105408 | tf_op jit(solution)/shard_map/all_gather | solution.py:403
  47.0 0.3 reshape.13.far_ref
  47.3 2.4 %causal.1 = bf16[128,2048]{1,0:T(8,128)(2,1)} custom-call(s32[1]{0:T(128)} %bitcast.refs_0_.me_ref, bf16[128,2048]{1,0:T(8,128)(2,1)S(1)} %get-tuple-element.9.q_ref, bf16[2032,256]{1,0:T(8,128)(2,1)S(1)} %reshape.13.far_ref, bf16[128,256]{1,0:T(8,128)(2,1)S(1)} %pad_maximum_fusion.own_ref), custom_call_target="tpu_custom_call" | custom-call | flops 2147483648 | bytes 3145728 | tf_op jit(solution)/shard_map/causal/pallas_call | solution.py:359
  (3 shorter events, 0.0 us)
Async XLA Ops:
  0.6 5.4 %copy-start.6 = (f32[2048]{0:T(1024)S(1)}, f32[2048]{0:T(1024)}, u32[]{:S(2)}) copy-start(f32[2048]{0:T(1024)} %param.8) | copy-start | bytes 24580
  0.6 9.2 %collective-permute-start = (bf16[128,512]{1,0:T(8,128)(2,1)}, bf16[128,512]{1,0:T(8,128)(2,1)S(1)}, u32[]{:S(2)}, u32[]{:S(2)}) collective-permute-start(bf16[128,512]{1,0:T(8,128)(2,1)} %refs_4_.3), channel_id=1, source_target_pairs={{0,1},{1,2},{2,3},{3,4},{4,5},{5,6},{6,7},{7,8},{8,9},{9,10},{10,1... | collective-permute-start | bytes 393224 | tf_op jit(solution)/shard_map/ppermute | solution.py:384
  6.1 1.2 %copy-start = (bf16[2048,256]{1,0:T(8,128)(2,1)S(1)}, bf16[2048,256]{1,0:T(8,128)(2,1)}, u32[]{:S(2)}) copy-start(bf16[2048,256]{1,0:T(8,128)(2,1)} %refs_6_.3) | copy-start | bytes 3145732
  7.3 1.0 %copy-start.2 = (bf16[128,2048]{1,0:T(8,128)(2,1)S(1)}, bf16[128,2048]{1,0:T(8,128)(2,1)}, u32[]{:S(2)}) copy-start(bf16[128,2048]{1,0:T(8,128)(2,1)} %refs_2_.3) | copy-start | bytes 1572868
  8.3 0.9 %copy-start.4 = (bf16[128,512]{1,0:T(8,128)(2,1)S(1)}, bf16[128,512]{1,0:T(8,128)(2,1)}, u32[]{:S(2)}) copy-start(bf16[128,512]{1,0:T(8,128)(2,1)} %refs_4_.3) | copy-start | bytes 393220
  9.2 1.2 %copy-start.1 = (bf16[2048,256]{1,0:T(8,128)(2,1)S(1)}, bf16[2048,256]{1,0:T(8,128)(2,1)}, u32[]{:S(2)}) copy-start(bf16[2048,256]{1,0:T(8,128)(2,1)} %refs_6_.3) | copy-start | bytes 3145732
  9.2 1.4 %copy-start.3 = (bf16[128,2048]{1,0:T(8,128)(2,1)S(1)}, bf16[128,2048]{1,0:T(8,128)(2,1)}, u32[]{:S(2)}) copy-start(bf16[128,2048]{1,0:T(8,128)(2,1)} %refs_2_.3) | copy-start | bytes 1572868
  9.2 1.4 %copy-start.5 = (bf16[128,512]{1,0:T(8,128)(2,1)S(1)}, bf16[128,512]{1,0:T(8,128)(2,1)}, u32[]{:S(2)}) copy-start(bf16[128,512]{1,0:T(8,128)(2,1)} %refs_4_.3) | copy-start | bytes 393220
  10.6 7.0 %copy-start.7 = (bf16[128,2048]{1,0:T(8,128)(2,1)S(1)}, bf16[128,2048]{1,0:T(8,128)(2,1)}, u32[]{:S(2)}) copy-start(bf16[128,2048]{1,0:T(8,128)(2,1)} %refs_8_.1) | copy-start | bytes 1572868
  15.6 7.4 %collective-permute-start.1 = (bf16[16,256]{1,0:T(8,128)(2,1)S(1)}, bf16[16,256]{1,0:T(8,128)(2,1)S(1)}, u32[]{:S(2)}, u32[]{:S(2)}) collective-permute-start(bf16[16,256]{1,0:T(8,128)(2,1)S(1)} %slice.3), channel_id=1, source_target_pairs={{0,1},{1,2},{2,3},{3,4},{4,5},{5,6},{6,7},{7,8},{8,9},{9,10},{10,1... | collective-permute-start | bytes 24584 | tf_op jit(solution)/shard_map/ppermute | solution.py:384

commit v7 on v6

--- a/solution.py
+++ b/solution.py
@@ -279,7 +279,7 @@
                 return own_ref[:, lanes]
             return far_ref[tile * DIM : (tile + 1) * DIM, lanes]
 
-        heads = max(1, min(4, shards // tiles))
+        heads = max(1, min(8, shards // tiles))
 
         def gather_queries(item):
             return jnp.concatenate([q_ref[:, lanes_of(item * heads + h)] for h in range(heads)], 0)
@@ -369,7 +369,7 @@
         out_shape=jax.ShapeDtypeStruct(att_query.shape, jnp.bfloat16),
         scratch_shapes=[
             pltpu.VMEM((2, tokens // DIM, rows, DIM), jnp.float32),
-            pltpu.VMEM((2, 4, rows, DIM), jnp.float32),
+            pltpu.VMEM((2, 8, rows, DIM), jnp.float32),
         ],
         compiler_params=pltpu.CompilerParams(vmem_limit_bytes=48 * 1024 * 1024),
         cost_estimate=pl.CostEstimate(

time: 50 us -> 49.7 us (level)
  no operation moved by 1% of the time
where the time goes in v7:
time: 49.7 us; the launch traced here: 49.4 us
  blocking collectives  23.9 us (48%)
  Pallas kernels  12.5 us (25%)
  starting transfers between devices  7.33 us (15%)
  local copies, waits for them, and re-layouts  4.24 us (9%)
  between operations  0.73 us (1%)
  waiting for transfers between devices  0.61 us (1%)
    all_gather x1, blocking collectives, per_device(): far = lax.all_gather(share, 'seq', axis=0, tiled=True)  23.9 us
    pallas_call x2, Pallas kernels, tri_call(): pl.pallas_call(kernel, grid=(1,), in_specs=in_specs, out_specs=[pl.BlockS...  10.4 us
    ppermute x2, starting transfers between devices, passed_along(): return lax.ppermute(block, axis, [(i, i + 1) for i in range(count - 1)])  7.33 us
    unnamed x17, local copies, waits for them, and re-layouts  4.24 us
    pallas_call x1, Pallas kernels, att_call(): pl.pallas_call(functools.partial(att_kernel, rows=rows), grid=(1,), in_sp...  2.08 us
  transfers between devices with their start and end apart: 2, of which 1 were waited for; matrix products, arithmetic and copies ran while one was open for 0% of the time, Pallas kernels for 11%

profile of v7, /device:TPU:1, one launch (start us, length us, event | category | flops | bytes accessed | tf_op | source)
XLA Modules:
  0.0 49.4 jit_solution(8460245632747902526)
XLA Ops:
  0.6 0.0 copy-start.6
  0.6 5.4 %collective-permute-start = (bf16[128,512]{1,0:T(8,128)(2,1)}, bf16[128,512]{1,0:T(8,128)(2,1)S(1)}, u32[]{:S(2)}, u32[]{:S(2)}) collective-permute-start(bf16[128,512]{1,0:T(8,128)(2,1)} %refs_4_.3), channel_id=1, source_target_pairs={{0,1},{1,2},{2,3},{3,4},{4,5},{5,6},{6,7},{7,8},{8,9},{9,10},{10,1... | collective-permute-start | bytes 393224 | tf_op jit(solution)/shard_map/ppermute | solution.py:384
  6.0 0.0 copy-done.6
  6.1 0.0 copy-start
  6.1 1.2 %copy-done = bf16[2048,256]{1,0:T(8,128)(2,1)S(1)} copy-done((bf16[2048,256]{1,0:T(8,128)(2,1)S(1)}, bf16[2048,256]{1,0:T(8,128)(2,1)}, u32[]{:S(2)}) %copy-start) | copy-done | bytes 1048600
  7.3 0.0 copy-start.2
  7.3 1.0 %copy-done.2 = bf16[128,2048]{1,0:T(8,128)(2,1)S(1)} copy-done((bf16[128,2048]{1,0:T(8,128)(2,1)S(1)}, bf16[128,2048]{1,0:T(8,128)(2,1)}, u32[]{:S(2)}) %copy-start.2) | copy-done | bytes 524312
  8.3 0.0 copy-start.4
  8.3 0.9 %copy-done.4 = bf16[128,512]{1,0:T(8,128)(2,1)S(1)} copy-done((bf16[128,512]{1,0:T(8,128)(2,1)S(1)}, bf16[128,512]{1,0:T(8,128)(2,1)}, u32[]{:S(2)}) %copy-start.4) | copy-done | bytes 131096
  9.2 0.0 copy-start.1
  9.2 0.0 copy-start.3
  9.2 0.0 copy-start.5
  9.2 0.6 %collective-permute-done.refs_3_ = bf16[128,512]{1,0:T(8,128)(2,1)S(1)} collective-permute-done((bf16[128,512]{1,0:T(8,128)(2,1)}, bf16[128,512]{1,0:T(8,128)(2,1)S(1)}, u32[]{:S(2)}, u32[]{:S(2)}) %collective-permute-start) | collective-permute-done | bytes 131104 | tf_op jit(solution)/shard_map/ppermute | solution.py:384
  9.8 0.6 %copy-done.1 = bf16[2048,256]{1,0:T(8,128)(2,1)S(1)} copy-done((bf16[2048,256]{1,0:T(8,128)(2,1)S(1)}, bf16[2048,256]{1,0:T(8,128)(2,1)}, u32[]{:S(2)}) %copy-start.1) | copy-done | bytes 1048600
  10.5 0.1 copy-done.3
  10.6 0.0 copy-done.5
  10.6 0.0 copy-start.7
  10.6 5.0 %tri_part.2 = (bf16[128,2048]{1,0:T(8,128)(2,1)}, bf16[64,256]{1,0:T(8,128)(2,1)S(1)}) custom-call(s32[1]{0:T(128)} %bitcast.refs_0_.me_ref, f32[8,128]{1,0:T(8,128)S(1)} %stage.1.refs_1_, bf16[128,2048]{1,0:T(8,128)(2,1)S(1)} %copy-done.3, bf16[128,512]{1,0:T(8,128)(2,1)S(1)} %collective-permute-done.refs_3_, bf16[128,512]{1,0:T(8,128)(2,1)S(1)} %copy-done.5, ...), custom_call_target="tpu_custom_call" | custom-call | flops 2147483648 | bytes 2097152 | tf_op jit(solution)/shard_map/tri_part/pallas_call | solution.py:210
  15.6 1.9 %collective-permute-start.1 = (bf16[16,256]{1,0:T(8,128)(2,1)S(1)}, bf16[16,256]{1,0:T(8,128)(2,1)S(1)}, u32[]{:S(2)}, u32[]{:S(2)}) collective-permute-start(bf16[16,256]{1,0:T(8,128)(2,1)S(1)} %slice.3), channel_id=1, source_target_pairs={{0,1},{1,2},{2,3},{3,4},{4,5},{5,6},{6,7},{7,8},{8,9},{9,10},{10,1... | collective-permute-start | bytes 24584 | tf_op jit(solution)/shard_map/ppermute | solution.py:384
  17.6 0.0 copy-done.7
  17.6 5.4 %tri_part.3 = (bf16[128,2048]{1,0:T(8,128)(2,1)}, bf16[64,256]{1,0:T(8,128)(2,1)S(1)}, bf16[128,2048]{1,0:T(8,128)(2,1)S(1)}) custom-call(s32[1]{0:T(128)} %bitcast.refs_0_.me_ref, f32[8,128]{1,0:T(8,128)S(1)} %stage.1.refs_1_, bf16[128,2048]{1,0:T(8,128)(2,1)S(1)} %copy-done.3, ...), custom_call_target="tpu_custom_call", output_to_operand_aliasing={{0}: (7, {})} | custom-call | flops 2147483648 | bytes 2097152 | tf_op jit(solution)/shard_map/tri_part/pallas_call | solution.py:210
  23.0 0.0 collective-permute-done.1
  23.0 0.1 fusion.2
  23.1 23.9 %all-gather = bf16[16,127,256]{2,1,0:T(8,128)(2,1)S(1)} all-gather(bf16[1,127,256]{2,1,0:T(8,128)(2,1)S(1)} %fusion.2), channel_id=1, replica_groups=mesh['dp'=32,'seq'=16] {'seq'}, dimensions={0}, use_global_device_ids=true | all-gather | bytes 1105408 | tf_op jit(solution)/shard_map/all_gather | solution.py:403
  47.0 0.3 reshape.13.far_ref
  47.3 2.1 %causal.1 = bf16[128,2048]{1,0:T(8,128)(2,1)} custom-call(s32[1]{0:T(128)} %bitcast.refs_0_.me_ref, bf16[128,2048]{1,0:T(8,128)(2,1)S(1)} %get-tuple-element.9.q_ref, bf16[2032,256]{1,0:T(8,128)(2,1)S(1)} %reshape.13.far_ref, bf16[128,256]{1,0:T(8,128)(2,1)S(1)} %pad_maximum_fusion.own_ref), custom_call_target="tpu_custom_call" | custom-call | flops 2147483648 | bytes 3145728 | tf_op jit(solution)/shard_map/causal/pallas_call | solution.py:359
  (3 shorter events, 0.0 us)
Async XLA Ops:
  0.6 5.4 %copy-start.6 = (f32[2048]{0:T(1024)S(1)}, f32[2048]{0:T(1024)}, u32[]{:S(2)}) copy-start(f32[2048]{0:T(1024)} %param.8) | copy-start | bytes 24580
  0.6 9.2 %collective-permute-start = (bf16[128,512]{1,0:T(8,128)(2,1)}, bf16[128,512]{1,0:T(8,128)(2,1)S(1)}, u32[]{:S(2)}, u32[]{:S(2)}) collective-permute-start(bf16[128,512]{1,0:T(8,128)(2,1)} %refs_4_.3), channel_id=1, source_target_pairs={{0,1},{1,2},{2,3},{3,4},{4,5},{5,6},{6,7},{7,8},{8,9},{9,10},{10,1... | collective-permute-start | bytes 393224 | tf_op jit(solution)/shard_map/ppermute | solution.py:384
  6.1 1.2 %copy-start = (bf16[2048,256]{1,0:T(8,128)(2,1)S(1)}, bf16[2048,256]{1,0:T(8,128)(2,1)}, u32[]{:S(2)}) copy-start(bf16[2048,256]{1,0:T(8,128)(2,1)} %refs_6_.3) | copy-start | bytes 3145732
  7.3 1.0 %copy-start.2 = (bf16[128,2048]{1,0:T(8,128)(2,1)S(1)}, bf16[128,2048]{1,0:T(8,128)(2,1)}, u32[]{:S(2)}) copy-start(bf16[128,2048]{1,0:T(8,128)(2,1)} %refs_2_.3) | copy-start | bytes 1572868
  8.3 0.9 %copy-start.4 = (bf16[128,512]{1,0:T(8,128)(2,1)S(1)}, bf16[128,512]{1,0:T(8,128)(2,1)}, u32[]{:S(2)}) copy-start(bf16[128,512]{1,0:T(8,128)(2,1)} %refs_4_.3) | copy-start | bytes 393220
  9.2 1.2 %copy-start.1 = (bf16[2048,256]{1,0:T(8,128)(2,1)S(1)}, bf16[2048,256]{1,0:T(8,128)(2,1)}, u32[]{:S(2)}) copy-start(bf16[2048,256]{1,0:T(8,128)(2,1)} %refs_6_.3) | copy-start | bytes 3145732
  9.2 1.4 %copy-start.3 = (bf16[128,2048]{1,0:T(8,128)(2,1)S(1)}, bf16[128,2048]{1,0:T(8,128)(2,1)}, u32[]{:S(2)}) copy-start(bf16[128,2048]{1,0:T(8,128)(2,1)} %refs_2_.3) | copy-start | bytes 1572868
  9.2 1.4 %copy-start.5 = (bf16[128,512]{1,0:T(8,128)(2,1)S(1)}, bf16[128,512]{1,0:T(8,128)(2,1)}, u32[]{:S(2)}) copy-start(bf16[128,512]{1,0:T(8,128)(2,1)} %refs_4_.3) | copy-start | bytes 393220
  10.6 7.0 %copy-start.7 = (bf16[128,2048]{1,0:T(8,128)(2,1)S(1)}, bf16[128,2048]{1,0:T(8,128)(2,1)}, u32[]{:S(2)}) copy-start(bf16[128,2048]{1,0:T(8,128)(2,1)} %refs_8_.1) | copy-start | bytes 1572868
  15.6 7.4 %collective-permute-start.1 = (bf16[16,256]{1,0:T(8,128)(2,1)S(1)}, bf16[16,256]{1,0:T(8,128)(2,1)S(1)}, u32[]{:S(2)}, u32[]{:S(2)}) collective-permute-start(bf16[16,256]{1,0:T(8,128)(2,1)S(1)} %slice.3), channel_id=1, source_target_pairs={{0,1},{1,2},{2,3},{3,4},{4,5},{5,6},{6,7},{7,8},{8,9},{9,10},{10,1... | collective-permute-start | bytes 24584 | tf_op jit(solution)/shard_map/ppermute | solution.py:384
